TPU v7x, 128 devices: a whole 4x4x4 slice. The times are simulated.
128 devices in a mesh: batch: 32 (over y, x, core), blk: 4 (over z).
Axes of the slice: x: 4, y: 4, z: 4, core: 2. Of those that a mesh axis runs over, the one named last changes fastest.
Arguments:
- stream: bfloat16 [32, 2040, 768], P('batch', 'blk'), may hold values from -6 to 6
- cotangent: bfloat16 [32, 2040, 768], P('batch', 'blk'), may hold values from -6 to 6
- passes: int32 [32], P('batch'), may hold values from 2 to 5
- w_qkv: bfloat16 [768, 2304], replicated, may hold values from -0.3125 to 0.3125
- w_out: bfloat16 [768, 768], replicated, may hold values from -0.625 to 0.625
- w_up: bfloat16 [768, 3072], replicated, may hold values from -0.21875 to 0.21875
- w_down: bfloat16 [3072, 768], replicated, may hold values from -0.109375 to 0.109375
- ln_gains: float32 [768, 2], replicated, may hold values from 0.5 to 1.5
- pass_embed: float32 [768, 5], replicated, may hold values from -3 to 3
Outputs:
- layer_out: bfloat16 [32, 2040, 768], P('batch', 'blk')
- grad_stream: float32 [32, 2040, 768], P('batch', 'blk')
- grad_qkv: float32 [768, 2304], P('blk')
- grad_out: float32 [768, 768], P('blk')
- grad_up: float32 [768, 3072], P('blk')
- grad_down: float32 [3072, 768], P('blk')
- grad_gains: float32 [768, 2], P('blk')
- grad_pass: float32 [768, 5], P('blk')
Inputs may be any that keep to these rules, and one draw needn't show every extreme that they name: `passes`: 2040 is a multiple of every sequence's pass count.
All inputs are finite; a program needn't handle non-finite values.
Results may differ from a plain program's by a relative error of at most 0.012.
Values may be sent and summed in bfloat16 or wider, within the bound.
No kernel may reach another device: no remote copies, remote signals or barrier semaphores. Data moves between devices by JAX's collectives and lax.ppermute only.
A program may use at most 320 MiB of HBM per device.

v0:
```python
import jax
import jax.numpy as jnp
from jax import lax
from jax.sharding import PartitionSpec as P

D = 768
HEADS = 12
HD = 64
PASSES = 5


HIGH = lax.Precision.HIGHEST
EPS = 1e-05


def layer_norm(values, gain):
    mean = jnp.mean(values, axis=-1, keepdims=True)
    centred = values - mean
    inverse = lax.rsqrt(jnp.mean(centred * centred, axis=-1, keepdims=True) + EPS)
    return centred * inverse * gain


def outer_sum(left, right):
    return lax.dot_general(
        left, right, (((0,), (0,)), ((), ())), preferred_element_type=jnp.float32
    )


def times_back(left, weight):
    return lax.dot_general(
        left, weight, (((1,), (1,)), ((), ())), preferred_element_type=jnp.float32
    )


def attention_probs(query_heads, kv_all, position):
    total = kv_all.shape[0]
    key_heads = kv_all[:, :D].reshape(total, HEADS, HD)
    raw = jnp.einsum("qhd,khd->hqk", query_heads, key_heads, preferred_element_type=jnp.float32)
    scaled = raw * HD ** (-0.5)
    allowed = position[:, None] >= jnp.arange(total, dtype=jnp.int32)[None, :]
    scaled = jnp.where(allowed[None], scaled, -1e30)
    top = jnp.max(scaled, axis=-1, keepdims=True)
    expd = jnp.exp(scaled - top)
    return expd / jnp.sum(expd, axis=-1, keepdims=True)


def on_device(stream, cotangent, passes, w_qkv, w_out, w_up, w_down, ln_gains, pass_embed):
    rows = stream.shape[1]
    position = lax.axis_index("blk") * rows + jnp.arange(rows, dtype=jnp.int32)
    which = position % passes[0]
    onehot = (which[:, None] == jnp.arange(PASSES, dtype=jnp.int32)[None, :]).astype(jnp.float32)
    hidden = stream[0].astype(jnp.float32) + jnp.einsum(
        "tp,dp->td", onehot, pass_embed, precision=HIGH
    )
    gain_one = ln_gains[:, 0]
    gain_two = ln_gains[:, 1]
    normed, norm_one_back = jax.vjp(layer_norm, hidden, gain_one)
    normed_low = normed.astype(jnp.bfloat16)
    qkv_low = jnp.dot(normed_low, w_qkv, preferred_element_type=jnp.float32).astype(jnp.bfloat16)
    query_heads = qkv_low[:, :D].reshape(rows, HEADS, HD)
    kv_all = lax.all_gather(qkv_low[:, D:], "blk", axis=0, tiled=True)
    probs = attention_probs(query_heads, kv_all, position)
    probs_low = probs.astype(jnp.bfloat16)
    total = kv_all.shape[0]
    value_heads = kv_all[:, D:].reshape(total, HEADS, HD)
    attended = jnp.einsum(
        "hqk,khd->qhd", probs_low, value_heads, preferred_element_type=jnp.float32
    )
    attended_low = attended.reshape(rows, D).astype(jnp.bfloat16)
    middle = hidden + jnp.dot(attended_low, w_out, preferred_element_type=jnp.float32)
    second, norm_two_back = jax.vjp(layer_norm, middle, gain_two)
    second_low = second.astype(jnp.bfloat16)
    upward = jnp.dot(second_low, w_up, preferred_element_type=jnp.float32)
    active, gelu_back = jax.vjp(jax.nn.gelu, upward)
    active_low = active.astype(jnp.bfloat16)
    layer_out = (middle + jnp.dot(active_low, w_down, preferred_element_type=jnp.float32)).astype(
        jnp.bfloat16
    )
    grad_top = cotangent[0]
    grad_down = outer_sum(active_low, grad_top)
    d_active = times_back(grad_top, w_down)
    d_upward = gelu_back(d_active)[0].astype(jnp.bfloat16)
    grad_up = outer_sum(second_low, d_upward)
    d_second = times_back(d_upward, w_up)
    d_middle_part, grad_gain_two = norm_two_back(d_second)
    d_middle = grad_top.astype(jnp.float32) + d_middle_part
    d_branch = d_middle.astype(jnp.bfloat16)
    grad_out = outer_sum(attended_low, d_branch)
    d_attended = times_back(d_branch, w_out).astype(jnp.bfloat16).reshape(rows, HEADS, HD)
    kv_back = lax.all_gather(qkv_low[:, D:], "blk", axis=0, tiled=True)
    probs_back = attention_probs(query_heads, kv_back, position)
    probs_back_low = probs_back.astype(jnp.bfloat16)
    key_back = kv_back[:, :D].reshape(total, HEADS, HD)
    value_back = kv_back[:, D:].reshape(total, HEADS, HD)
    d_probs = jnp.einsum("qhd,khd->hqk", d_attended, value_back, preferred_element_type=jnp.float32)
    spread = jnp.sum(probs_back * d_probs, axis=-1, keepdims=True)
    d_scores = (probs_back * (d_probs - spread) * HD ** (-0.5)).astype(jnp.bfloat16)
    d_query = jnp.einsum("hqk,khd->qhd", d_scores, key_back, preferred_element_type=jnp.float32)
    d_query_low = d_query.reshape(rows, D).astype(jnp.bfloat16)
    d_key_term = jnp.einsum(
        "hqk,qhd->khd", d_scores, query_heads, preferred_element_type=jnp.float32
    )
    d_value_term = jnp.einsum(
        "hqk,qhd->khd", probs_back_low, d_attended, preferred_element_type=jnp.float32
    )
    kv_term = jnp.concatenate(
        [d_key_term.reshape(total, D), d_value_term.reshape(total, D)], axis=1
    )
    kv_grad = lax.psum_scatter(kv_term, "blk", scatter_dimension=0, tiled=True).astype(jnp.bfloat16)
    d_qkv = jnp.concatenate([d_query_low, kv_grad], axis=1)
    grad_qkv = outer_sum(normed_low, d_qkv)
    d_normed = times_back(d_qkv, w_qkv)
    d_hidden_part, grad_gain_one = norm_one_back(d_normed)
    grad_stream = d_middle + d_hidden_part
    grad_pass = jnp.einsum("td,tp->dp", grad_stream, onehot, precision=HIGH)
    grad_gains = jnp.stack([grad_gain_one, grad_gain_two], axis=1)
    terms = (grad_qkv, grad_out, grad_up, grad_down, grad_gains, grad_pass)
    shards = (
        lax.psum_scatter(terms[0], "blk", scatter_dimension=0, tiled=True),
        lax.psum_scatter(terms[1], "blk", scatter_dimension=0, tiled=True),
        lax.psum_scatter(terms[2], "blk", scatter_dimension=0, tiled=True),
        lax.psum_scatter(terms[3], "blk", scatter_dimension=0, tiled=True),
        lax.psum_scatter(terms[4], "blk", scatter_dimension=0, tiled=True),
        lax.psum_scatter(terms[5], "blk", scatter_dimension=0, tiled=True),
    )
    shards = lax.psum((shards[0], shards[1], shards[2], shards[3], shards[4], shards[5]), "batch")
    return (
        layer_out[None],
        grad_stream[None],
        shards[0],
        shards[1],
        shards[2],
        shards[3],
        shards[4],
        shards[5],
    )


def solution(mesh):
    in_specs = (
        P("batch", "blk", None),
        P("batch", "blk", None),
        P("batch"),
        P(),
        P(),
        P(),
        P(),
        P(),
        P(),
    )
    out_specs = (
        P("batch", "blk", None),
        P("batch", "blk", None),
        P("blk", None),
        P("blk", None),
        P("blk", None),
        P("blk", None),
        P("blk", None),
        P("blk", None),
    )
    return jax.shard_map(
        on_device, mesh=mesh, in_specs=in_specs, out_specs=out_specs, check_vma=False
    )
```

profile of v0, /device:TPU:1, one launch (start us, length us, event | category | flops | bytes accessed | tf_op | source)
XLA Modules:
  0.0 1024.1 jit_solution(2166475529491024632)
XLA Ops:
  24.5 61.9 %all-gather.3.cloned.1.call-done = bf16[4,510,1536]{2,1,0:T(8,128)(2,1)} async-done(((bf16[1,510,1536]{2,1,0:T(8,128)(2,1)}), bf16[4,510,1536]{2,1,0:T(8,128)(2,1)}) %all-gather.3.cloned.1.call-update) | async-done | bytes 6266896 | tf_op jit(solution)/shard_map/all_gather | solution.py:61
  86.4 7.1 reshape.144
  93.5 5.8 fusion.62
  109.3 26.2 %fusion.64 = (f32[12,510]{1,0:T(8,128)}, f32[12,510,2040]{1,2,0:T(8,128)}) fusion(pred[510,2040]{0,1:T(8,128)(4,1)} %iota_compare_fusion, bf16[510,12,64]{0,2,1:T(8,128)(2,1)} %bitcast.82, bf16[2040,12,64]{0,2,1:T(8,128)(2,1)} %bitcast.76), kind=kOutput, calls=%fused_computation.95 | convolution fusion | flops 1647995904 | bytes 54920880 | tf_op jit(solution)/shard_map/sub | solution.py:43
  135.5 17.9 %fusion.30 = bf16[12,64,510]{2,1,0:T(8,128)(2,1)S(1)} fusion(bf16[2040,12,64]{0,2,1:T(8,128)(2,1)} %bitcast.70, f32[12,510,2040]{1,2,0:T(8,128)} %get-tuple-element.53, f32[12,510]{1,0:T(8,128)} %get-tuple-element.52), kind=kOutput, calls=%fused_computation.53 | convolution fusion | flops 1623415680 | bytes 53880480 | tf_op jit(solution)/shard_map/hqk,khd->qhd/dot_general | solution.py:66
  154.7 5.2 fusion.58
  160.0 6.3 fusion.25
  177.0 20.6 %fusion.15 = f32[12,64,2040]{2,1,0:T(8,128)} fusion(bf16[510,12,64]{0,2,1:T(8,128)(2,1)} %bitcast.74, f32[12,510,2040]{1,2,0:T(8,128)} %get-tuple-element.53, f32[12,510]{1,0:T(8,128)} %get-tuple-element.52), kind=kOutput, calls=%fused_computation.15 | convolution fusion | flops 1623024000 | bytes 57013920 | tf_op jit(solution)/shard_map/hqk,qhd->khd/dot_general | solution.py:103
  197.6 21.4 %fusion.66 = f32[12,510,2040]{1,2,0:T(8,128)} fusion(bf16[510,12,64]{0,2,1:T(8,128)(2,1)} %bitcast.75, bf16[2040,12,64]{0,2,1:T(8,128)(2,1)} %bitcast.71), kind=kOutput, calls=%fused_computation.97 | convolution fusion | flops 1598054400 | bytes 53856000 | tf_op jit(solution)/shard_map/qhd,khd->hqk/dot_general | solution.py:95
  219.0 64.7 %fusion.10 = f32[12,64,2040]{2,1,0:T(8,128)} fusion(bf16[510,12,64]{0,2,1:T(8,128)(2,1)} %bitcast.83, f32[12,510,2040]{1,2,0:T(8,128)} %fusion.66, f32[12,510,2040]{1,2,0:T(8,128)} %get-tuple-element.53, f32[12,510]{1,0:T(8,128)} %get-tuple-element.52), kind=kOutput, calls=%fused_computation.12 | convolution fusion | flops 1685456128 | bytes 106953120 | tf_op jit(solution)/shard_map/hqk,qhd->khd/dot_general | solution.py:100
  283.7 11.3 %pad_maximum_fusion = f32[2040,1536]{0,1:T(8,128)} fusion(f32[2040,768]{0,1:T(8,128)} %bitcast.72, f32[2040,768]{0,1:T(8,128)} %bitcast.73), kind=kLoop, calls=%fused_computation.14 | loop fusion | flops 3133440 | bytes 25067520 | tf_op jit(solution)/shard_map/concatenate | solution.py:106
  295.0 215.8 %all-reduce.7 = bf16[2040,1536]{0,1:T(8,128)(2,1)} all-reduce(f32[2040,1536]{0,1:T(8,128)} %pad_maximum_fusion), channel_id=2, replica_groups=mesh['batch'=32,'blk'=4] {'blk'}, use_global_device_ids=true, to_apply=%region_9.10.clone | all-reduce | flops 3133440 | bytes 18800640
  514.3 63.6 %fusion.33 = bf16[12,64,510]{2,1,0:T(8,128)(2,1)} fusion(bf16[2040,12,64]{0,2,1:T(8,128)(2,1)} %bitcast.77, f32[12,510,2040]{1,2,0:T(8,128)} %fusion.66, f32[12,510,2040]{1,2,0:T(8,128)} %get-tuple-element.53, f32[12,510]{1,0:T(8,128)} %get-tuple-element.52), kind=kOutput, calls=%fused_computation.54 | convolution fusion | flops 1685847808 | bytes 103819680 | tf_op jit(solution)/shard_map/hqk,khd->qhd/dot_general | solution.py:98
  577.9 7.3 fusion.28
  585.5 9.8 fusion.38
  596.0 9.6 fusion.57
  606.3 6.1 multiply_reduce_fusion.2
  624.0 33.9 %reduce-scatter.12.cloned.1.call-done = f32[192,2304]{1,0:T(8,128)} async-done(((f32[768,2304]{1,0:T(8,128)}), f32[192,2304]{1,0:T(8,128)}) %reduce-scatter.12.cloned.1.call-update) | async-done | bytes 1769488 | tf_op jit(solution)/shard_map/reduce_scatter | solution.py:119
  657.9 91.1 %reduce-scatter.18.cloned.1.call-done = f32[768,768]{1,0:T(8,128)} async-done(((f32[3072,768]{1,0:T(8,128)}), f32[768,768]{1,0:T(8,128)}) %reduce-scatter.18.cloned.1.call-update) | async-done | bytes 2359312 | tf_op jit(solution)/shard_map/reduce_scatter | solution.py:122
  749.0 91.1 %reduce-scatter.16.cloned.1.call-done = f32[192,3072]{1,0:T(8,128)} async-done(((f32[768,3072]{1,0:T(8,128)}), f32[192,3072]{1,0:T(8,128)}) %reduce-scatter.16.cloned.1.call-update) | async-done | bytes 2359312 | tf_op jit(solution)/shard_map/reduce_scatter | solution.py:121
  845.5 8.8 fusion.36
  854.3 7.3 reduce-scatter.20.cloned.1.call-done
  862.5 22.4 %reduce-scatter.22.cloned.1.call-done = f32[192,5]{1,0:T(8,128)} async-done(((f32[768,5]{1,0:T(8,128)}), f32[192,5]{1,0:T(8,128)}) %reduce-scatter.22.cloned.1.call-update) | async-done | bytes 3856
  885.8 124.3 %all-reduce.1 = (f32[192,2]{0,1:T(2,128)}, f32[192,5]{0,1:T(8,128)}) all-reduce(f32[192,2]{0,1:T(2,128)S(1)} %copy.37, f32[192,5]{0,1:T(8,128)S(1)} %copy.39), channel_id=1, replica_groups=mesh['batch'=32,'blk'=4] {'batch'}, use_global_device_ids=true, to_apply=%region_23.24 | all-reduce | flops 1344 | bytes 10752 | tf_op jit(solution)/shard_map/psum | solution.py:126
  (135 shorter events, 68.1 us)
Async XLA Ops:
  7.2 79.3 %all-gather.3.cloned.1.call-start = ((), (), s32[]{:S(2)}) async-start(), calls=%async_computation.10 | async-start | bytes 7864320 | tf_op jit(solution)/shard_map/all_gather | solution.py:61
  9.0 5.5 copy-start.13
  9.0 160.8 %copy-start.15 = (f32[768]{0:T(1024)}, f32[768]{0:T(1024)S(1)}, u32[]{:S(2)}) copy-start(f32[768]{0:T(1024)S(1)} %get-tuple-element.36) | copy-start | bytes 9220
  17.2 606.8 %reduce-scatter.14.cloned.1.call-start = ((), (), s32[]{:S(2)}) async-start(), calls=%async_computation.7 | async-start | bytes 2949120 | tf_op jit(solution)/shard_map/reduce_scatter | solution.py:120
  135.4 18.0 %copy-start.2 = (f32[510,768]{1,0:T(8,128)S(1)}, f32[510,768]{1,0:T(8,128)}, u32[]{:S(2)}) copy-start(f32[510,768]{1,0:T(8,128)} %copy-done.1) | copy-start | bytes 4700164
  135.5 18.0 %copy-start.11 = (bf16[768,768]{1,0:T(8,128)(2,1)S(1)}, bf16[768,768]{1,0:T(8,128)(2,1)}, u32[]{:S(2)}) copy-start(bf16[768,768]{1,0:T(8,128)(2,1)} %param.13) | copy-start | bytes 3538948
  153.4 6.6 slice-start.2
  154.3 15.5 %copy-start.3 = (f32[510,768]{1,0:T(8,128)}, f32[510,768]{1,0:T(8,128)S(1)}, u32[]{:S(2)}) copy-start(f32[510,768]{1,0:T(8,128)S(1)} %get-tuple-element.55) | copy-start | bytes 4700164
  154.4 15.5 %copy-start.19 = (f32[510]{0:T(512)}, f32[510]{0:T(512)S(1)}, u32[]{:S(2)}) copy-start(f32[510]{0:T(512)S(1)} %broadcast_multiply_fusion) | copy-start | bytes 6124
  154.7 15.1 %copy-start.24 = (f32[510]{0:T(512)}, f32[510]{0:T(512)S(1)}, u32[]{:S(2)}) copy-start(f32[510]{0:T(512)S(1)} %fusion.48) | copy-start | bytes 6124
  154.7 11.6 %slice-start = ((s8[4718592]{0:T(1024)(128)(4,1)}), s8[4194304]{0:T(1024)(128)(4,1)S(1)}, s32[]{:S(2)}) async-start(s8[4718592]{0:T(1024)(128)(4,1)} %bitcast.84), calls=%async_computation.14 | async-start | bytes 8388608
  160.0 6.3 copy-start.31
  160.0 6.3 slice-start.1
  219.0 438.9 %reduce-scatter.12.cloned.1.call-start = ((), (), s32[]{:S(2)}) async-start(), calls=%async_computation.6 | async-start | bytes 8847360 | tf_op jit(solution)/shard_map/reduce_scatter | solution.py:119
  514.3 63.6 %copy-start.14 = (f32[768]{0:T(1024)S(1)}, f32[768]{0:T(1024)}, u32[]{:S(2)}) copy-start(f32[768]{0:T(1024)} %copy-done.13) | copy-start | bytes 9220
  514.3 63.6 %copy-start.18 = (f32[510]{0:T(512)S(1)}, f32[510]{0:T(512)}, u32[]{:S(2)}) copy-start(f32[510]{0:T(512)} %copy-done.17) | copy-start | bytes 6124
  514.3 63.6 %copy-start.22 = (f32[510]{0:T(512)S(1)}, f32[510]{0:T(512)}, u32[]{:S(2)}) copy-start(f32[510]{0:T(512)} %copy-done.21) | copy-start | bytes 6124
  585.2 163.8 %reduce-scatter.18.cloned.1.call-start = ((), (), s32[]{:S(2)}) async-start(), calls=%async_computation.9 | async-start | bytes 11796480 | tf_op jit(solution)/shard_map/reduce_scatter | solution.py:122
  595.3 244.8 %reduce-scatter.16.cloned.1.call-start = ((), (), s32[]{:S(2)}) async-start(), calls=%async_computation.8 | async-start | bytes 11796480 | tf_op jit(solution)/shard_map/reduce_scatter | solution.py:121
  605.7 255.9 %reduce-scatter.20.cloned.1.call-start = ((), (), s32[]{:S(2)}) async-start(), calls=%async_computation.11 | async-start | bytes 491520
  612.4 6.6 copy-start.26
  618.9 266.0 %reduce-scatter.22.cloned.1.call-start = ((), (), s32[]{:S(2)}) async-start(), calls=%async_computation.12 | async-start | bytes 491520
  623.6 386.5 %all-reduce.6.cloned.1.call-start = ((), (), s32[]{:S(2)}) async-start(), calls=%async_computation.13 | async-start | bytes 14155776 | tf_op jit(solution)/shard_map/psum | solution.py:126
  840.2 5.3 copy-start.4
  (20 other events, 52.2 us)
Sparse Core Ops, SparseCore 0:
  17.3 69.0 all-gather.2
  219.1 32.6 reduce-scatter.13
  585.3 72.4 reduce-scatter.11
  660.2 88.7 reduce-scatter.17
  751.3 88.7 reduce-scatter.15
  843.0 18.5 reduce-scatter.19
  864.0 20.7 reduce-scatter.21
  888.6 119.7 all-reduce.5
where the time goes:
time: 1030 us; the launch traced here: 1020 us
  blocking collectives  340 us (33%)
  waiting for transfers between devices  308 us (30%)
  matrix products  285 us (28%)
  local copies, waits for them, and re-layouts  52.2 us (5%)
  other arithmetic  22 us (2%)
  between operations  16.6 us (2%)
    unnamed x1, blocking collectives  216 us
    psum x1, blocking collectives, on_device(): lax.psum((shards[0], shards[1], shards[2], shards[3], shards[4], shards[5...  124 us
    reduce_scatter x1, waiting for transfers between devices, on_device(): lax.psum_scatter(terms[3], 'blk', scatter_dimension=0, tiled=True)  91.1 us
    reduce_scatter x1, waiting for transfers between devices, on_device(): lax.psum_scatter(terms[2], 'blk', scatter_dimension=0, tiled=True)  91.1 us
    dot_general x1, matrix products, on_device(): jnp.einsum('hqk,qhd->khd', d_scores, query_heads, preferred_element_type=...  64.7 us
    dot_general x1, matrix products, on_device(): jnp.einsum('hqk,khd->qhd', d_scores, key_back, preferred_element_type=jnp...  63.6 us
    all_gather x1, waiting for transfers between devices, on_device(): kv_all = lax.all_gather(qkv_low[:, D:], 'blk', axis=0, tiled=True)  61.9 us
    reduce_scatter x1, waiting for transfers between devices, on_device(): lax.psum_scatter(terms[0], 'blk', scatter_dimension=0, tiled=True)  33.9 us
  transfers between devices with their start and end apart: 8, of which 6 were waited for; matrix products, arithmetic and copies ran while one was open for 20% of the time, Pallas kernels for 0%

commit v1 on v0

v1 whole, which is shorter than its diff:
```python
import jax
import jax.numpy as jnp
from jax import lax
from jax.experimental import pallas as pl
from jax.experimental.pallas import tpu as pltpu
from jax.sharding import PartitionSpec as P

D = 768
HEADS = 12
HD = 64
FF = 3072
PASSES = 5
ROWS = 510
R = 512
EPS = 1e-05
NEG = -1e30
BF = jnp.bfloat16
F32 = jnp.float32
VM = pl.BlockSpec(memory_space=pltpu.VMEM)
SM = pl.BlockSpec(memory_space=pltpu.SMEM)
HB = pl.BlockSpec(memory_space=pl.ANY)
PARAMS = pltpu.CompilerParams(vmem_limit_bytes=56 * 1024 * 1024)


def shape(dims, kind=BF):
    return jax.ShapeDtypeStruct(dims, kind)


def dot(left, right):
    return jnp.dot(left, right, preferred_element_type=F32)


def dot_nt(left, right):
    return lax.dot_general(left, right, (((1,), (1,)), ((), ())), preferred_element_type=F32)


def normalize(values):
    mean = jnp.mean(values, axis=-1, keepdims=True)
    centred = values - mean
    inverse = lax.rsqrt(jnp.mean(centred * centred, axis=-1, keepdims=True) + EPS)
    return centred * inverse, inverse


def norm_back(grad, unit, inverse, gain):
    scaled = grad * gain
    first = jnp.mean(scaled, axis=-1, keepdims=True)
    second = jnp.mean(scaled * unit, axis=-1, keepdims=True)
    return inverse * (scaled - first - unit * second)


def pass_index(blk, count):
    row = lax.broadcasted_iota(jnp.int32, (R, 1), 0) + blk * ROWS
    turns = jnp.floor((row.astype(F32) + 0.5) / count.astype(F32)).astype(jnp.int32)
    return row - turns * count


def pieces_out(stage, outs, blk):
    for d, out in enumerate(outs):
        out[...] = stage[lax.rem(blk + d, 4)]


def project(normed, weights, stage, outs, blk):
    for part, weight in enumerate(weights):
        got = dot(normed, weight[...])
        if part == 0:
            got = got.astype(BF) * jnp.asarray(HD ** (-0.5), BF)
        turned = got.astype(BF).T
        for j in range(4):
            stage[j, 64 * part : 64 * part + 64, :] = turned[64 * j : 64 * j + 64]
    pieces_out(stage, outs, blk)


def first_kernel(blk_ref, count_ref, stream, embed, gains, wq, wk, wv, hidden, normed, turned, p0, p1, p2, p3, stage):
    blk = blk_ref[0]
    hidden[R - 8 : R, :] = jnp.zeros((8, D), F32)
    hidden[0:ROWS, :] = stream[0].astype(F32)
    which = pass_index(blk, count_ref[0])
    added = embed[0:1, :]
    for r in range(1, PASSES):
        added = jnp.where(which == r, embed[r : r + 1, :], added)
    values = hidden[...] + added
    hidden[...] = values
    unit, _ = normalize(values)
    row = lax.broadcasted_iota(jnp.int32, (R, 1), 0)
    low = jnp.where(row < ROWS, unit * gains[0:1, :], 0.0).astype(BF)
    normed[...] = low
    project(low, (wq, wk, wv), stage, (p0, p1, p2, p3), blk)
    turned[...] = low.T


def second_kernel(blk_ref, normed, wq1, wk1, wv1, wq2, wk2, wv2, a0, a1, a2, a3, b0, b1, b2, b3, stage, stage2):
    blk = blk_ref[0]
    low = normed[...]
    project(low, (wq1, wk1, wv1), stage, (a0, a1, a2, a3), blk)
    project(low, (wq2, wk2, wv2), stage2, (b0, b1, b2, b3), blk)


def load_heads(blk, parts, q_rows, k_rows, v_rows, k_cols):
    for d in range(4):
        s = lax.rem(blk + 4 - d, 4)
        piece = parts[d]
        q_rows[s, 0:64, :] = piece[0:64, :]
        k_rows[s, 0:64, :] = piece[64:128, :]
        v_rows[s] = piece[128:192, :]
    row = lax.broadcasted_iota(jnp.int32, (64, R), 0)
    col = lax.broadcasted_iota(jnp.int32, (64, R), 1)
    one = jnp.where(row == 0, 1.0, 0.0).astype(BF)
    off = jnp.where((row == 0) & (col >= ROWS), NEG, 0.0).astype(BF)
    for s in range(4):
        q_rows[s, 64:128, :] = one
        k_rows[s, 64:128, :] = off
    for s in range(4):
        k_cols[s] = k_rows[s].T


def causal():
    key = lax.broadcasted_iota(jnp.int32, (R, R), 0)
    query = lax.broadcasted_iota(jnp.int32, (R, R), 1)
    return key <= query


def attend_kernel(blk_ref, r0, r1, r2, r3, p0, p1, p2, p3, attended, spread, q_rows, k_rows, v_rows, k_cols, scores, stage):
    blk = blk_ref[0]
    load_heads(blk, (r0, r1, r2, r3), q_rows, k_rows, v_rows, k_cols)
    for i in range(4):
        top = None
        for j in range(i + 1):
            got = dot(k_cols[j], q_rows[i])
            if i == j:
                got = jnp.where(causal(), got, NEG)
            scores[j] = got
            best = jnp.max(got, axis=0, keepdims=True)
            top = best if top is None else jnp.maximum(top, best)
        total = jnp.zeros((1, R), F32)
        summed = jnp.zeros((HD, R), F32)
        for j in range(i + 1):
            raised = jnp.exp(scores[j] - top)
            total = total + jnp.sum(raised, axis=0, keepdims=True)
            summed = summed + dot(v_rows[j], raised.astype(BF))
        result = summed / total
        attended[i] = result
        spread[i] = top + jnp.log(total)
        stage[i] = result.astype(BF)
    pieces_out(stage, (p0, p1, p2, p3), blk)


def attend_back_kernel(
    last, blk_ref, r0, r1, r2, r3, g0, g1, g2, g3, attended, spread, a0, a1, a2, a3, *rest
):
    if last:
        prev0, prev1, p0, p1, p2, p3, grad, q_rows, k_rows, v_rows, k_cols, q_cols, v_cols, o_rows, o_cols, delta, dq, outs = rest
    else:
        p0, p1, p2, p3, grad, q_rows, k_rows, v_rows, k_cols, q_cols, v_cols, o_rows, o_cols, delta, dq, outs = rest
    blk = blk_ref[0]
    load_heads(blk, (r0, r1, r2, r3), q_rows, k_rows, v_rows, k_cols)
    for d, piece in enumerate((g0, g1, g2, g3)):
        o_rows[lax.rem(blk + 4 - d, 4)] = piece[...]
    for s in range(4):
        q_cols[s] = q_rows[s].T
        v_cols[s] = v_rows[s].T
        o_cols[s] = o_rows[s].T
        delta[s] = jnp.sum(o_rows[s].astype(F32) * attended[s], axis=0, keepdims=True)
        dq[s] = jnp.zeros((HD, R), F32)
    for j in range(4):
        dk = jnp.zeros((R, 2 * HD), F32)
        dv = jnp.zeros((R, HD), F32)
        for i in range(j, 4):
            got = dot(k_cols[j], q_rows[i])
            if i == j:
                got = jnp.where(causal(), got, NEG)
            probs = jnp.exp(got - spread[i])
            d_probs = dot(v_cols[j], o_rows[i])
            d_scores = (probs * (d_probs - delta[i])).astype(BF)
            dv = dv + dot(probs.astype(BF), o_cols[i])
            dk = dk + dot(d_scores, q_cols[i])
            dq[i] = dq[i] + dot(k_rows[j, 0:64, :], d_scores)
        outs[j, 0:64, :] = (dq[j] * HD ** (-0.5)).astype(BF)
        outs[j, 64:128, :] = dk[:, 0:64].astype(BF).T
        outs[j, 128:192, :] = dv.astype(BF).T
        outs[j, 192:256, :] = jnp.zeros((64, R), BF)
    for d, out in enumerate((p0, p1, p2, p3)):
        out[...] = outs[lax.rem(blk + d, 4), 0:192, :]
    made = jnp.zeros((D, 256), F32)
    for d, piece in enumerate((a0, a1, a2, a3)):
        s = lax.rem(blk + 4 - d, 4)
        made = made + dot(piece[...], outs[s].T)
    if last:
        grad[:, 0:192] = prev0[...]
        grad[:, 192:384] = prev1[...]
        grad[:, 384:576] = made[:, 0:192].astype(BF)
    else:
        grad[...] = made[:, 0:192].astype(BF)


def gelu_both(value):
    c = (2.0 / jnp.pi) ** 0.5
    square = value * value
    t = jnp.tanh(c * value * (1.0 + 0.044715 * square))
    cdf = 0.5 * (1.0 + t)
    slope = cdf + (0.5 * c) * value * (1.0 - t * t) * (1.0 + 3.0 * 0.044715 * square)
    return value * cdf, slope


CHUNK = 512


def ff_kernel(
    blk_ref, r0, r1, r2, r3, hidden, cot, gains, w_out, w_up, w_down,
    active, d_up, second, middle, o_turned, d_branch, d_middle, gain_term, p0, p1, p2, p3,
    dy, back, stage,
):
    step = pl.program_id(0)

    @pl.when(step == 0)
    def _():
        blk = blk_ref[0]
        for d, piece in enumerate((r0, r1, r2, r3)):
            s = lax.rem(blk + 4 - d, 4)
            for g in range(3):
                stage[4 * g + s] = piece[64 * g : 64 * g + 64, :]
        o_rows = stage[...].reshape(D, R)
        o_turned[...] = o_rows
        values = hidden[...] + dot(o_rows.T, w_out[...])
        middle[...] = values
        unit, _ = normalize(values)
        second[...] = (unit * gains[1:2, :]).astype(BF)
        back[R - 8 : R, :] = jnp.zeros((8, D), F32)
        back[0:ROWS, :] = cot[0].astype(F32)
        dy[...] = back[...].astype(BF)
        back[...] = jnp.zeros((R, D), F32)

    upward = dot(second[...], w_up[...])
    act, slope = gelu_both(upward)
    active[...] = act.astype(BF)
    d_active = dot_nt(dy[...], w_down[...])
    d_upward = (d_active * slope).astype(BF)
    d_up[...] = d_upward
    back[...] += dot_nt(d_upward, w_up[...])

    @pl.when(step == FF // CHUNK - 1)
    def _():
        blk = blk_ref[0]
        unit, inverse = normalize(middle[...])
        grad = back[...]
        gain_term[...] = jnp.sum(grad * unit, axis=0, keepdims=True)
        total = dy[...].astype(F32) + norm_back(grad, unit, inverse, gains[1:2, :])
        d_middle[...] = total
        low = total.astype(BF)
        d_branch[...] = low
        stage[...] = dot_nt(w_out[...], low).astype(BF).reshape(HEADS, HD, R)
        for d, out in enumerate((p0, p1, p2, p3)):
            j = lax.rem(blk + d, 4)
            for g in range(3):
                out[64 * g : 64 * g + 64, :] = stage[4 * g + j]


def ff_grad_kernel(sel_ref, active, d_up, second, cot, o_turned, d_branch, up_out, down_out, out_out, dy, second_turned, pad):
    step = pl.program_id(0)

    @pl.when(step == 0)
    def _():
        pad[R - 8 : R, :] = jnp.zeros((8, D), F32)
        pad[0:ROWS, :] = cot[0].astype(F32)
        dy[...] = pad[...].astype(BF)
        second_turned[...] = second[...].T
        half = dot(o_turned[...], d_branch[...]).astype(BF)
        for i in range(4):
            for n in range(16):
                if n < 12:
                    out_out[n // 4, n % 4, i] = half[192 * i + 16 * n : 192 * i + 16 * n + 16, :]
                else:
                    out_out[n // 4, n % 4, i] = jnp.zeros((16, 384), BF)

    up = dot(second_turned[...], d_up[...]).astype(BF)
    for i in range(4):
        for yy in range(4):
            up_out[yy, 0, i] = up[192 * i + 48 * yy : 192 * i + 48 * yy + 48, :]
    down = dot(active[...].T, dy[...]).astype(BF)
    for yy in range(4):
        for xx in range(4):
            r = 48 * (2 * yy + xx // 2)
            down_out[yy, xx, 0] = down[r : r + 48, 384 * (xx % 2) : 384 * (xx % 2) + 384]


def layer_out_kernel(middle, active, w_down, out, total):
    step = pl.program_id(0)

    @pl.when(step == 0)
    def _():
        total[...] = middle[...]

    total[...] += dot(active[...], w_down[...])

    @pl.when(step == FF // CHUNK - 1)
    def _():
        out[0] = total[0:ROWS, :].astype(BF)


def last_kernel(
    blk_ref, count_ref, a0, a1, a2, a3, b0, b1, b2, b3, c0, c1, c2, c3, hidden, d_middle, gain_term, gains, w_qkv,
    grad_stream, small, stage,
):
    blk = blk_ref[0]
    for g, group in enumerate(((a0, a1, a2, a3), (b0, b1, b2, b3), (c0, c1, c2, c3))):
        for d, piece in enumerate(group):
            s = lax.rem(blk + 4 - d, 4)
            for part in range(3):
                stage[12 * part + 4 * g + s] = piece[64 * part : 64 * part + 64, :]
    grad = dot(w_qkv[...], stage[...].reshape(3 * D, R)).T
    unit, inverse = normalize(hidden[...])
    total = d_middle[...] + norm_back(grad, unit, inverse, gains[0:1, :])
    grad_stream[0] = total[0:ROWS, :]
    row = lax.broadcasted_iota(jnp.int32, (R, 1), 0)
    which = jnp.where(row < ROWS, pass_index(blk, count_ref[0]), -1)
    small[0:1, :] = jnp.sum(grad * unit, axis=0, keepdims=True)
    small[1:2, :] = gain_term[...]
    for r in range(PASSES):
        small[2 + r : 3 + r, :] = jnp.sum(jnp.where(which == r, total, 0.0), axis=0, keepdims=True)
    small[7:8, :] = jnp.zeros((1, D), F32)


def shift(values, axis, d):
    if axis == "z":
        return lax.ppermute(values, "blk", [(i, (i + d) % 4) for i in range(4)])
    pairs = []
    for b in range(32):
        y, x, core = b // 8, (b // 2) % 4, b % 2
        if axis == "y":
            y = (y + d) % 4
        elif axis == "x":
            x = (x + d) % 4
        else:
            core = (core + d) % 2
        pairs.append((b, 8 * y + 2 * x + core))
    return lax.ppermute(values, "batch", pairs)


def spread_pieces(pieces, axis):
    return (pieces[0],) + tuple(shift(pieces[d], axis, d) for d in (1, 2, 3))


def pick(values, index, dim):
    return lax.dynamic_index_in_dim(values, index, dim, keepdims=False)


def scatter_sum(terms, where, axis, dim):
    pieces = []
    for d in range(4):
        index = lax.rem(where + d, 4)
        pieces.append(sum(pick(t, index, dim).astype(F32) for t in terms).astype(BF))
    return spread_pieces(pieces, axis)


def add(terms):
    return sum(t.astype(F32) for t in terms)


def sum_four(values, axis):
    one, two, three = (shift(values, axis, d).astype(F32) for d in (1, 2, 3))
    return (values.astype(F32) + two) + (one + three)


def gather(piece, where, axis):
    got = jnp.stack((piece,) + tuple(shift(piece, axis, d) for d in (1, 2, 3)))
    return jnp.take(got, lax.rem(where + 4 - jnp.arange(4, dtype=jnp.int32), 4), axis=0)


def gather_core(piece, core):
    other = shift(piece, "core", 1)
    return jnp.where(core == 0, jnp.stack((piece, other)), jnp.stack((other, piece)))


def weight_spec(column):
    return pl.BlockSpec((D, 256), lambda *_, column=column: (0, column))


def on_device(stream, cotangent, passes, w_qkv, w_out, w_up, w_down, ln_gains, pass_embed):
    z = lax.axis_index("blk")
    batch = lax.axis_index("batch")
    core, x, y = batch % 2, (batch // 2) % 4, batch // 8
    blk = z.astype(jnp.int32).reshape(1)
    gains = ln_gains.T
    embed = pass_embed.T
    piece = shape((192, R))
    full = shape((R, D))

    hidden, normed, turned, *sent = pl.pallas_call(
        first_kernel,
        grid=(1,),
        in_specs=[SM, SM, VM, VM, VM, weight_spec(0), weight_spec(3), weight_spec(6)],
        out_specs=[VM] * 7,
        out_shape=[shape((R, D), F32), full, shape((D, R))] + [piece] * 4,
        scratch_shapes=[pltpu.VMEM((4, 192, R), BF)],
        compiler_params=PARAMS,
        name="ln_qkv_first",
    )(blk, passes, stream, embed, gains, w_qkv, w_qkv, w_qkv)
    heads = [spread_pieces(sent, "z")]
    sent = pl.pallas_call(
        second_kernel,
        grid=(1,),
        in_specs=[SM, VM] + [weight_spec(c) for c in (1, 4, 7, 2, 5, 8)],
        out_specs=[VM] * 8,
        out_shape=[piece] * 8,
        scratch_shapes=[pltpu.VMEM((4, 192, R), BF)] * 2,
        compiler_params=PARAMS,
        name="qkv_rest",
    )(blk, normed, *([w_qkv] * 6))
    heads += [spread_pieces(sent[:4], "z"), spread_pieces(sent[4:], "z")]

    attended, spreads, sent = [], [], []
    for g in range(3):
        *parts, result, spread = pl.pallas_call(
            attend_kernel,
            in_specs=[SM] + [VM] * 4,
            out_specs=[VM] * 6,
            out_shape=[shape((HD, R))] * 4 + [shape((4, HD, R), F32), shape((4, 1, R), F32)],
            scratch_shapes=[
                pltpu.VMEM((4, 128, R), BF),
                pltpu.VMEM((4, 128, R), BF),
                pltpu.VMEM((4, HD, R), BF),
                pltpu.VMEM((4, R, 128), BF),
                pltpu.VMEM((4, R, R), F32),
                pltpu.VMEM((4, HD, R), BF),
            ],
            compiler_params=PARAMS,
            name="attend",
        )(blk, *heads[g])
        attended.append(result)
        spreads.append(spread)
        sent.append(parts)
    back_o = spread_pieces([jnp.concatenate([sent[g][d] for g in range(3)], axis=0) for d in range(4)], "z")
    turned_all = spread_pieces((turned, turned, turned, turned), "z")

    whole = pl.BlockSpec(memory_space=pltpu.VMEM)
    active, d_up, second, middle, o_turned, d_branch, d_middle, gain_term, *sent = pl.pallas_call(
        ff_kernel,
        grid=(FF // CHUNK,),
        in_specs=[SM] + [VM] * 4 + [VM, VM, VM, VM]
        + [pl.BlockSpec((D, CHUNK), lambda f: (0, f)), pl.BlockSpec((CHUNK, D), lambda f: (f, 0))],
        out_specs=[pl.BlockSpec((R, CHUNK), lambda f: (0, f)), pl.BlockSpec((R, CHUNK), lambda f: (0, f))] + [whole] * 10,
        out_shape=[shape((R, FF)), shape((R, FF)), full, shape((R, D), F32), shape((D, R)), full, shape((R, D), F32), shape((1, D), F32)]
        + [piece] * 4,
        scratch_shapes=[pltpu.VMEM((R, D), BF), pltpu.VMEM((R, D), F32), pltpu.VMEM((HEADS, HD, R), BF)],
        compiler_params=PARAMS,
        name="ff",
    )(blk, *back_o, hidden, cotangent, gains, w_out, w_up, w_down)
    d_o = spread_pieces(sent, "z")

    def ff_grads(select):
        return pl.pallas_call(
            ff_grad_kernel,
            grid_spec=pltpu.PrefetchScalarGridSpec(
                num_scalar_prefetch=1,
                grid=(4,),
                in_specs=[
                    pl.BlockSpec((R, 384), lambda i, s: (0, 2 * i + s[0])),
                    pl.BlockSpec((R, 384), lambda i, s: (0, 2 * i + s[0])),
                    pl.BlockSpec((R, D), lambda i, s: (0, 0)),
                    pl.BlockSpec((1, ROWS, D), lambda i, s: (0, 0, 0)),
                    pl.BlockSpec((D, R), lambda i, s: (0, 0)),
                    pl.BlockSpec((R, 384), lambda i, s: (0, s[0])),
                ],
                out_specs=[
                    pl.BlockSpec((4, 1, 4, 48, 384), lambda i, s: (0, i, 0, 0, 0)),
                    pl.BlockSpec((4, 4, 1, 48, 384), lambda i, s: (0, 0, i, 0, 0)),
                    pl.BlockSpec((4, 4, 4, 16, 384), lambda i, s: (0, 0, 0, 0, 0)),
                ],
                scratch_shapes=[pltpu.VMEM((R, D), BF), pltpu.VMEM((D, R), BF), pltpu.VMEM((R, D), F32)],
            ),
            out_shape=[shape((4, 4, 4, 48, 384)), shape((4, 4, 4, 48, 384)), shape((4, 4, 4, 16, 384))],
            compiler_params=PARAMS,
            name="ff_grad",
        )(select, active, d_up, second, cotangent, o_turned, d_branch)

    core_index = core.astype(jnp.int32).reshape(1)
    other = ff_grads(1 - core_index)
    swapped = [shift(t, "core", 1) for t in other]
    mine = ff_grads(core_index)
    layer_out = pl.pallas_call(
        layer_out_kernel,
        grid=(FF // CHUNK,),
        in_specs=[VM, pl.BlockSpec((R, CHUNK), lambda f: (0, f)), pl.BlockSpec((CHUNK, D), lambda f: (f, 0))],
        out_specs=VM,
        out_shape=shape((1, ROWS, D)),
        scratch_shapes=[pltpu.VMEM((R, D), F32)],
        compiler_params=PARAMS,
        name="layer_out",
    )(middle, active, w_down)

    a_terms = scatter_sum((mine[0], swapped[0]), x, "x", 1)
    b_terms = scatter_sum((mine[1], swapped[1]), y, "y", 0)
    c_terms = scatter_sum((mine[2], swapped[2]), y, "y", 0)
    a_terms = scatter_sum(a_terms, y, "y", 0)
    b_terms = scatter_sum(b_terms, x, "x", 0)
    c_terms = scatter_sum(c_terms, x, "x", 0)
    bulk = [jnp.concatenate([a, b, c], axis=1) for a, b, c in zip(a_terms, b_terms, c_terms)]
    bulk = add(scatter_sum(bulk, z, "z", 0)).astype(BF)
    bulk = gather(gather(bulk, y, "y"), x, "x")
    bulk = gather_core(bulk, core).astype(F32)
    up, down, out = bulk[..., 0:48, :], bulk[..., 48:96, :], bulk[..., 96:112, :]
    grad_up = up.transpose(2, 3, 1, 0, 4).reshape(192, FF)
    down = down.reshape(2, 2, 2, 4, 48, 384)
    grad_down = down.transpose(0, 3, 1, 4, 2, 5).reshape(D, D)
    grad_out = out[:, :, 0:3].transpose(2, 1, 3, 0, 4).reshape(192, D)

    pieces, grads = [], []
    for g in range(3):
        last = g == 2
        *sent, grad = pl.pallas_call(
            lambda *refs, last=last: attend_back_kernel(last, *refs),
            grid=(1,),
            in_specs=[SM] + [VM] * 4 + [pl.BlockSpec((HD, R), lambda _, g=g: (g, 0))] * 4 + [VM] * 6 + [VM] * (2 if last else 0),
            out_specs=[VM] * 5,
            out_shape=[piece] * 4 + [shape((D, 576 if last else 192))],
            scratch_shapes=[
                pltpu.VMEM((4, 128, R), BF),
                pltpu.VMEM((4, 128, R), BF),
                pltpu.VMEM((4, HD, R), BF),
                pltpu.VMEM((4, R, 128), BF),
                pltpu.VMEM((4, R, 128), BF),
                pltpu.VMEM((4, R, HD), BF),
                pltpu.VMEM((4, HD, R), BF),
                pltpu.VMEM((4, R, HD), BF),
                pltpu.VMEM((4, 1, R), F32),
                pltpu.VMEM((4, HD, R), F32),
                pltpu.VMEM((4, 256, R), BF),
            ],
            compiler_params=PARAMS,
            name="attend_back",
        )(blk, *heads[g], *d_o, attended[g], spreads[g], *turned_all, *(grads if last else ()))
        grads.append(grad)
        pieces.extend(spread_pieces(sent, "z"))

    grad_stream, small = pl.pallas_call(
        last_kernel,
        in_specs=[SM, SM] + [VM] * 17,
        out_specs=[VM, VM],
        out_shape=[shape((1, ROWS, D), F32), shape((8, D), F32)],
        scratch_shapes=[pltpu.VMEM((36, HD, R), BF)],
        compiler_params=PARAMS,
        name="ln_back",
    )(blk, passes, *pieces, hidden, d_middle, gain_term, gains, w_qkv)

    made = grads[2].reshape(4, 2, 4, 24, 576)
    terms = (pick(made, core, 1), shift(pick(made, 1 - core, 1), "core", 1))
    terms = scatter_sum(terms, x, "x", 1)
    mid = add(terms).astype(BF)
    mid = sum_four(mid, "y").astype(BF)
    got = spread_pieces([pick(mid, lax.rem(z + d, 4), 0) for d in range(4)], "z")
    got = jnp.stack(got)
    got = gather_core(gather(got, x, "x"), core)
    got = jnp.take(got, lax.rem(z + 4 - jnp.arange(4, dtype=jnp.int32), 4), axis=2)
    got = got.reshape(2, 4, 4, 24, 3, 3, HD).transpose(0, 1, 3, 5, 4, 2, 6)
    grad_qkv = got.reshape(192, 3 * D).astype(F32)

    for axis in ("core", "x", "y", "z"):
        if axis == "core":
            small = small + shift(small, axis, 1)
        else:
            small = sum_four(small, axis)
    small = lax.dynamic_slice_in_dim(small.T, 192 * z, 192, 0)
    return (
        layer_out,
        grad_stream,
        grad_qkv,
        grad_out,
        grad_up,
        grad_down,
        small[:, 0:2],
        small[:, 2:7],
    )


def solution(mesh):
    tokens = P("batch", "blk", None)
    in_specs = (tokens, tokens, P("batch"), P(), P(), P(), P(), P(), P())
    out_specs = (tokens, tokens) + (P("blk", None),) * 6
    return jax.shard_map(on_device, mesh=mesh, in_specs=in_specs, out_specs=out_specs, check_vma=False)
```

time: 1030 us -> 430 us (0.42)
  blocking collectives: 340 us -> 0 us
  matrix products: 285 us -> 0 us
  waiting for transfers between devices: 308 us -> 138 us
  starting transfers between devices: 0.87 us -> 118 us
  Pallas kernels: 0 us -> 114 us
  local copies, waits for them, and re-layouts: 52.2 us -> 29.7 us
  between operations: 16.6 us -> 2.43 us
    dot_general x18 -> x0, matrix products: 254 us -> none  [the longest x1 64.7 us: on_device(): jnp.einsum('hqk,qhd->khd', d_scores, query_heads, preferred_element_type=...]
    reduce_scatter x4 -> x0, waiting for transfers between devices: 216 us -> none  [the longest x1 91.1 us: on_device(): lax.psum_scatter(terms[3], 'blk', scatter_dimension=0, tiled=True)]
    unnamed x1 -> x0, blocking collectives: 216 us -> none
    ppermute x0 -> x82, waiting for transfers between devices: none -> 138 us  [the longest x36 80 us: shift(): return lax.ppermute(values, 'blk', [(i, (i + d) % 4) for i in range(4)])]
    psum x1 -> x0, blocking collectives: 124 us -> none  [on_device(): lax.psum((shards[0], shards[1], shards[2], shards[3], shards[4], shards[5...]
    ppermute x0 -> x82, starting transfers between devices: none -> 118 us  [the longest x46 79.3 us: shift(): return lax.ppermute(values, 'batch', pairs)]
    pallas_call x0 -> x13, Pallas kernels: none -> 114 us  [the longest x3 34.7 us: on_device(): pl.pallas_call(lambda *refs, last=last: attend_back_kernel(last, *refs),...]
    all_gather x1 -> x0, waiting for transfers between devices: 61.9 us -> none  [on_device(): kv_all = lax.all_gather(qkv_low[:, D:], 'blk', axis=0, tiled=True)]
  transfers between devices with their start and end apart: 8 -> 82, of which waited for: 6 -> 39; matrix products, arithmetic and copies ran while one was open for 20% -> 8% of each run, Pallas kernels for 0% -> 17%
where the time goes in v1:
time: 430 us; the launch traced here: 424 us
  waiting for transfers between devices  138 us (32%)
  starting transfers between devices  118 us (27%)
  Pallas kernels  114 us (27%)
  local copies, waits for them, and re-layouts  29.7 us (7%)
  other arithmetic  22.3 us (5%)
    ppermute x36, waiting for transfers between devices, shift(): return lax.ppermute(values, 'blk', [(i, (i + d) % 4) for i in range(4)])  80 us
    ppermute x46, starting transfers between devices, shift(): return lax.ppermute(values, 'batch', pairs)  79.3 us
    ppermute x46, waiting for transfers between devices, shift(): return lax.ppermute(values, 'batch', pairs)  58.5 us
    ppermute x36, starting transfers between devices, shift(): return lax.ppermute(values, 'blk', [(i, (i + d) % 4) for i in range(4)])  38.5 us
    pallas_call x3, Pallas kernels, on_device(): pl.pallas_call(lambda *refs, last=last: attend_back_kernel(last, *refs),...  34.7 us
    pallas_call x1, Pallas kernels, on_device(): pl.pallas_call(ff_kernel, grid=(FF // CHUNK,), in_specs=[SM] + [VM] * 4 +...  18.7 us
    pallas_call x3, Pallas kernels, on_device(): pl.pallas_call(attend_kernel, in_specs=[SM] + [VM] * 4, out_specs=[VM] *...  18 us
    pallas_call x2, Pallas kernels, ff_grads(): pl.pallas_call(ff_grad_kernel, grid_spec=pltpu.PrefetchScalarGridSpec(num...  16.6 us
  transfers between devices with their start and end apart: 82, of which 39 were waited for; matrix products, arithmetic and copies ran while one was open for 8% of the time, Pallas kernels for 17%

profile of v1, /device:TPU:1, one launch (start us, length us, event | category | flops | bytes accessed | tf_op | source)
XLA Modules:
  0.0 424.1 jit_solution(15044249783862106134)
XLA Ops:
  5.6 4.4 %qkv_rest.1 = (bf16[192,512]{1,0:T(8,128)(2,1)}, bf16[192,512]{1,0:T(8,128)(2,1)}, bf16[192,512]{1,0:T(8,128)(2,1)}, bf16[192,512]{1,0:T(8,128)(2,1)}, bf16[192,...) custom-call(s32[1]{0:T(128)} %bitcast.blk_ref.refs_0_, ...), custom_call_target="tpu_custom_call" | custom-call | tf_op jit(solution)/shard_map/qkv_rest/pallas_call | solution.py:398
  29.6 6.0 %attend.4 = (bf16[64,512]{1,0:T(8,128)(2,1)}, bf16[64,512]{1,0:T(8,128)(2,1)}, bf16[64,512]{1,0:T(8,128)(2,1)}, bf16[64,512]{1,0:T(8,128)(2,1)}, f32[4,64,512]{2,1,0:T(8,128)}, /*index=5*/f32[4,1,512]{2,1,0:T(1,128)}) custom-call(s32[1]{0:T(128)} %bitcast.blk_ref.refs_0_, bf16[192,512]{1,0:T(8,128)(2,1)} %get-tuple-element.82.r0.refs_1_, ...), custom_call_target="tpu_custom_call" | custom-call | tf_op jit(solution)/shard_map/attend/pallas_call | solution.py:412
  36.4 6.0 %attend.5 = (bf16[64,512]{1,0:T(8,128)(2,1)}, bf16[64,512]{1,0:T(8,128)(2,1)}, bf16[64,512]{1,0:T(8,128)(2,1)}, bf16[64,512]{1,0:T(8,128)(2,1)}, f32[4,64,512]{2,1,0:T(8,128)}, /*index=5*/f32[4,1,512]{2,1,0:T(1,128)}) custom-call(s32[1]{0:T(128)} %bitcast.blk_ref.refs_0_, bf16[192,512]{1,0:T(8,128)(2,1)} %get-tuple-element.87.r0.refs_1_, ...), custom_call_target="tpu_custom_call" | custom-call | tf_op jit(solution)/shard_map/attend/pallas_call | solution.py:412
  43.3 6.0 %attend.3 = (bf16[64,512]{1,0:T(8,128)(2,1)}, bf16[64,512]{1,0:T(8,128)(2,1)}, bf16[64,512]{1,0:T(8,128)(2,1)}, bf16[64,512]{1,0:T(8,128)(2,1)}, f32[4,64,512]{2,1,0:T(8,128)}, /*index=5*/f32[4,1,512]{2,1,0:T(1,128)}) custom-call(s32[1]{0:T(128)} %bitcast.blk_ref.refs_0_, bf16[192,512]{1,0:T(8,128)(2,1)} %get-tuple-element.76.r0.refs_1_, ...), custom_call_target="tpu_custom_call" | custom-call | tf_op jit(solution)/shard_map/attend/pallas_call | solution.py:412
  61.6 18.7 %ff.1 = (bf16[512,3072]{1,0:T(8,128)(2,1)}, bf16[512,3072]{1,0:T(8,128)(2,1)}, bf16[512,768]{1,0:T(8,128)(2,1)}, f32[512,768]{1,0:T(8,128)}, bf16[768,512]{1,0:T...) custom-call(s32[1]{0:T(128)} %bitcast.blk_ref.refs_0_, ...), custom_call_target="tpu_custom_call" | custom-call | tf_op jit(solution)/shard_map/ff/pallas_call | solution.py:435
  80.3 8.4 %ff_grad.3 = (bf16[4,4,4,48,384]{4,3,2,1,0:T(8,128)(2,1)}, bf16[4,4,4,48,384]{4,3,2,1,0:T(8,128)(2,1)}, bf16[4,4,4,16,384]{4,3,2,1,0:T(8,128)(2,1)}) custom-call(s32[1]{0:T(128)S(6)} %sub.85.sel_ref, bf16[512,3072]{1,0:T(8,128)(2,1)} %get-tuple-element.103.active, bf16[512,3072]{1,0:T(8,128)(2,1)} %get-tuple-element.133.d_up, ...), custom_call_target="tpu_custom_call" | custom-call | tf_op jit(solution)/shard_map/ff_grad/pallas_call | solution.py:450
  88.7 7.2 %collective-permute-start.41 = (bf16[4,4,4,48,384]{4,3,2,1,0:T(8,128)(2,1)}, bf16[4,4,4,48,384]{4,3,2,1,0:T(8,128)(2,1)}, u32[]{:S(2)}, u32[]{:S(2)}) collective-permute-start(bf16[4,4,4,48,384]{4,3,2,1,0:T(8,128)(2,1)} %get-tuple-element.138), channel_id=1, source_target_pairs={{0,4},{4,0},{8,12},{12,8},{16,20},{20,16},{24,28},{28,24},{32,36},... | collective-permute-start | bytes 7077896 | tf_op jit(solution)/shard_map/ppermute | solution.py:335
  103.6 36.8 %collective-permute-done.13.refs_7_ = bf16[192,512]{1,0:T(8,128)(2,1)S(1)} collective-permute-done((bf16[192,512]{1,0:T(8,128)(2,1)S(1)}, bf16[192,512]{1,0:T(8,128)(2,1)S(1)}, u32[]{:S(2)}, u32[]{:S(2)}) %collective-permute-start.13) | collective-permute-done | bytes 196640 | tf_op jit(solution)/shard_map/ppermute | solution.py:324
  140.4 5.5 %collective-permute-done.14.refs_8_ = bf16[192,512]{1,0:T(8,128)(2,1)S(1)} collective-permute-done((bf16[192,512]{1,0:T(8,128)(2,1)S(1)}, bf16[192,512]{1,0:T(8,128)(2,1)S(1)}, u32[]{:S(2)}, u32[]{:S(2)}) %collective-permute-start.14) | collective-permute-done | bytes 196640 | tf_op jit(solution)/shard_map/ppermute | solution.py:324
  149.3 11.2 %attend_back.4 = (bf16[192,512]{1,0:T(8,128)(2,1)}, bf16[192,512]{1,0:T(8,128)(2,1)}, bf16[192,512]{1,0:T(8,128)(2,1)}, bf16[192,512]{1,0:T(8,128)(2,1)}, bf16[768,192]{1,0:T(8,128)(2,1)}) custom-call(s32[1]{0:T(128)} %bitcast.blk_ref.refs_0_, bf16[192,512]{1,0:T(8,128)(2,1)} %get-tuple-element.82.r0.refs_1_, bf16[192,512]{1,0:T(8,128)(2,1)} %copy-done.14, ...), custom_call_target="tpu_custom_call" | custom-call | tf_op jit(solution)/shard_map/attend_back/pallas_call | solution.py:509
  160.6 11.7 %attend_back.3 = (bf16[192,512]{1,0:T(8,128)(2,1)}, bf16[192,512]{1,0:T(8,128)(2,1)}, bf16[192,512]{1,0:T(8,128)(2,1)}, bf16[192,512]{1,0:T(8,128)(2,1)}, bf16[768,192]{1,0:T(8,128)(2,1)}) custom-call(s32[1]{0:T(128)} %bitcast.blk_ref.refs_0_, bf16[192,512]{1,0:T(8,128)(2,1)} %get-tuple-element.76.r0.refs_1_, bf16[192,512]{1,0:T(8,128)(2,1)} %copy-done.17, ...), custom_call_target="tpu_custom_call" | custom-call | tf_op jit(solution)/shard_map/attend_back/pallas_call | solution.py:509
  172.3 11.7 %attend_back.5 = (bf16[192,512]{1,0:T(8,128)(2,1)}, bf16[192,512]{1,0:T(8,128)(2,1)}, bf16[192,512]{1,0:T(8,128)(2,1)}, bf16[192,512]{1,0:T(8,128)(2,1)}, bf16[768,576]{1,0:T(8,128)(2,1)}) custom-call(s32[1]{0:T(128)} %bitcast.blk_ref.refs_0_, bf16[192,512]{1,0:T(8,128)(2,1)} %get-tuple-element.87.r0.refs_1_, bf16[192,512]{1,0:T(8,128)(2,1)} %copy-done.11, ...), custom_call_target="tpu_custom_call" | custom-call | tf_op jit(solution)/shard_map/attend_back/pallas_call | solution.py:509
  187.7 4.5 %collective-permute-done.24.c1 = bf16[192,512]{1,0:T(8,128)(2,1)S(1)} collective-permute-done((bf16[192,512]{1,0:T(8,128)(2,1)}, bf16[192,512]{1,0:T(8,128)(2,1)S(1)}, u32[]{:S(2)}, u32[]{:S(2)}) %collective-permute-start.24) | collective-permute-done | bytes 196640 | tf_op jit(solution)/shard_map/ppermute | solution.py:324
  199.6 4.6 %collective-permute-done.22.b2 = bf16[192,512]{1,0:T(8,128)(2,1)S(1)} collective-permute-done((bf16[192,512]{1,0:T(8,128)(2,1)}, bf16[192,512]{1,0:T(8,128)(2,1)S(1)}, u32[]{:S(2)}, u32[]{:S(2)}) %collective-permute-start.22) | collective-permute-done | bytes 196640 | tf_op jit(solution)/shard_map/ppermute | solution.py:324
  214.2 8.6 %ln_back.1 = (f32[1,510,768]{2,1,0:T(8,128)}, f32[8,768]{1,0:T(8,128)}) custom-call(s32[1]{0:T(128)} %bitcast.blk_ref.refs_0_, s32[1]{0:T(128)S(6)} %copy.54.count_ref, bf16[192,512]{1,0:T(8,128)(2,1)} %get-tuple-element.111.a0, bf16[192,512]{1,0:T(8,128)(2,1)} %copy-done.33, bf16[192,512]{1,0:T(8,128)(2,1)} %copy-done.34, bf16[192,512]{1,0:T(8,128)(2,1)} %copy-done.35, ...), custom_call_target="tpu_custom_call" | custom-call | tf_op jit(solution)/shard_map/ln_back/pallas_call | solution.py:534
  222.8 8.1 %collective-permute-start.72 = (f32[8,768]{1,0:T(8,128)}, f32[8,768]{1,0:T(8,128)S(1)}, u32[]{:S(2)}, u32[]{:S(2)}) collective-permute-start(f32[8,768]{1,0:T(8,128)} %get-tuple-element.143), channel_id=1, source_target_pairs={{0,4},{4,0},{8,12},{12,8},{16,20},{20,16},{24,28},{28,24},{32,36},... | collective-permute-start | bytes 73736 | tf_op jit(solution)/shard_map/ppermute | solution.py:335
  242.2 8.2 %ff_grad.2 = (bf16[4,4,4,48,384]{4,3,2,1,0:T(8,128)(2,1)}, bf16[4,4,4,48,384]{4,3,2,1,0:T(8,128)(2,1)}, bf16[4,4,4,16,384]{4,3,2,1,0:T(8,128)(2,1)}) custom-call(s32[1]{0:T(128)} %bitcast.29.sel_ref, bf16[512,3072]{1,0:T(8,128)(2,1)} %get-tuple-element.103.active, bf16[512,3072]{1,0:T(8,128)(2,1)} %get-tuple-element.133.d_up, ...), custom_call_target="tpu_custom_call" | custom-call | tf_op jit(solution)/shard_map/ff_grad/pallas_call | solution.py:450
  270.5 4.4 %collective-permute-done.50 = bf16[4,4,16,384]{3,2,1,0:T(8,128)(2,1)S(1)} collective-permute-done((bf16[4,4,16,384]{3,2,1,0:T(8,128)(2,1)S(1)}, bf16[4,4,16,384]{3,2,1,0:T(8,128)(2,1)S(1)}, u32[]{:S(2)}, u32[]{:S(2)}) %collective-permute-start.50) | collective-permute-done | bytes 196640 | tf_op jit(solution)/shard_map/ppermute | solution.py:335
  287.1 4.4 %collective-permute-done.43 = bf16[4,4,48,384]{3,2,1,0:T(8,128)(2,1)S(1)} collective-permute-done((bf16[4,4,48,384]{3,2,1,0:T(8,128)(2,1)S(1)}, bf16[4,4,48,384]{3,2,1,0:T(8,128)(2,1)S(1)}, u32[]{:S(2)}, u32[]{:S(2)}) %collective-permute-start.43) | collective-permute-done | bytes 589856 | tf_op jit(solution)/shard_map/ppermute | solution.py:335
  291.8 11.3 %collective-permute-done.44 = bf16[4,4,48,384]{3,2,1,0:T(8,128)(2,1)S(1)} collective-permute-done((bf16[4,4,48,384]{3,2,1,0:T(8,128)(2,1)S(1)}, bf16[4,4,48,384]{3,2,1,0:T(8,128)(2,1)S(1)}, u32[]{:S(2)}, u32[]{:S(2)}) %collective-permute-start.44) | collective-permute-done | bytes 589856 | tf_op jit(solution)/shard_map/ppermute | solution.py:335
  308.4 10.1 %collective-permute-done.53 = bf16[4,48,384]{2,1,0:T(8,128)(2,1)S(1)} collective-permute-done((bf16[4,48,384]{2,1,0:T(8,128)(2,1)S(1)}, bf16[4,48,384]{2,1,0:T(8,128)(2,1)S(1)}, u32[]{:S(2)}, u32[]{:S(2)}) %collective-permute-start.53) | collective-permute-done | bytes 147488 | tf_op jit(solution)/shard_map/ppermute | solution.py:335
  358.2 5.7 %collective-permute-done.68 = bf16[4,112,384]{2,1,0:T(8,128)(2,1)S(1)} collective-permute-done((bf16[4,112,384]{2,1,0:T(8,128)(2,1)S(1)}, bf16[4,112,384]{2,1,0:T(8,128)(2,1)S(1)}, u32[]{:S(2)}, u32[]{:S(2)}) %collective-permute-start.68) | collective-permute-done | bytes 344096 | tf_op jit(solution)/shard_map/ppermute | solution.py:335
  369.8 18.9 %collective-permute-start.71 = (bf16[4,4,112,384]{3,2,1,0:T(8,128)(2,1)}, bf16[4,4,112,384]{3,2,1,0:T(8,128)(2,1)}, u32[]{:S(2)}, u32[]{:S(2)}) collective-permute-start(bf16[4,4,112,384]{3,2,1,0:T(8,128)(2,1)} %broadcast_select_fusion), channel_id=1, source_target_pairs={{0,4},{4,0},{8,12},{12,8},{16,20},{20,16},{24,28},{28,24},{32,36},... | collective-permute-start | bytes 4128776 | tf_op jit(solution)/shard_map/ppermute | solution.py:335
  388.9 8.1 %layer_out.1 = bf16[1,510,768]{2,1,0:T(8,128)(2,1)} custom-call(f32[512,768]{1,0:T(8,128)} %get-tuple-element.102.middle, bf16[512,3072]{1,0:T(8,128)(2,1)} %get-tuple-element.103.active, bf16[3072,768]{1,0:T(8,128)(2,1)} %w_down.3), custom_call_target="tpu_custom_call" | custom-call | tf_op jit(solution)/shard_map/layer_out/pallas_call | solution.py:479
  (327 shorter events, 191.1 us)
Async XLA Ops:
  17.3 18.3 %collective-permute-start.7 = (bf16[192,512]{1,0:T(8,128)(2,1)}, bf16[192,512]{1,0:T(8,128)(2,1)S(1)}, u32[]{:S(2)}, u32[]{:S(2)}) collective-permute-start(bf16[192,512]{1,0:T(8,128)(2,1)} %get-tuple-element.89), channel_id=1, source_target_pairs={{0,2},{1,3},{2,0},{3,1},{4,6},{5,7},{6,4},{7,5},{8,10},{9,11},{10,... | collective-permute-start | bytes 589832 | tf_op jit(solution)/shard_map/ppermute | solution.py:324
  19.4 16.2 %collective-permute-start.8 = (bf16[192,512]{1,0:T(8,128)(2,1)}, bf16[192,512]{1,0:T(8,128)(2,1)S(1)}, u32[]{:S(2)}, u32[]{:S(2)}) collective-permute-start(bf16[192,512]{1,0:T(8,128)(2,1)} %get-tuple-element.90), channel_id=1, source_target_pairs={{0,3},{1,0},{2,1},{3,2},{4,7},{5,4},{6,5},{7,6},{8,11},{9,8},{10,9... | collective-permute-start | bytes 589832 | tf_op jit(solution)/shard_map/ppermute | solution.py:324
  24.6 17.8 %collective-permute-start = (bf16[192,512]{1,0:T(8,128)(2,1)S(1)}, bf16[192,512]{1,0:T(8,128)(2,1)S(1)}, u32[]{:S(2)}, u32[]{:S(2)}) collective-permute-start(bf16[192,512]{1,0:T(8,128)(2,1)S(1)} %copy-done.47), channel_id=1, source_target_pairs={{0,1},{1,2},{2,3},{3,0},{4,5},{5,6},{6,7},{7,4},{8,9},{9,10},{10,1... | collective-permute-start | bytes 589832 | tf_op jit(solution)/shard_map/ppermute | solution.py:324
  24.7 17.8 %collective-permute-start.1 = (bf16[192,512]{1,0:T(8,128)(2,1)S(1)}, bf16[192,512]{1,0:T(8,128)(2,1)S(1)}, u32[]{:S(2)}, u32[]{:S(2)}) collective-permute-start(bf16[192,512]{1,0:T(8,128)(2,1)S(1)} %copy-done.46), channel_id=1, source_target_pairs={{0,2},{1,3},{2,0},{3,1},{4,6},{5,7},{6,4},{7,5},{8,10},{9,11},{10,... | collective-permute-start | bytes 589832 | tf_op jit(solution)/shard_map/ppermute | solution.py:324
  27.9 14.6 %collective-permute-start.2 = (bf16[192,512]{1,0:T(8,128)(2,1)S(1)}, bf16[192,512]{1,0:T(8,128)(2,1)S(1)}, u32[]{:S(2)}, u32[]{:S(2)}) collective-permute-start(bf16[192,512]{1,0:T(8,128)(2,1)S(1)} %copy-done.45), channel_id=1, source_target_pairs={{0,3},{1,0},{2,1},{3,2},{4,7},{5,4},{6,5},{7,6},{8,11},{9,8},{10,9... | collective-permute-start | bytes 589832 | tf_op jit(solution)/shard_map/ppermute | solution.py:324
  88.7 166.2 %collective-permute-start.41 = (bf16[4,4,4,48,384]{4,3,2,1,0:T(8,128)(2,1)}, bf16[4,4,4,48,384]{4,3,2,1,0:T(8,128)(2,1)}, u32[]{:S(2)}, u32[]{:S(2)}) collective-permute-start(bf16[4,4,4,48,384]{4,3,2,1,0:T(8,128)(2,1)} %get-tuple-element.138), channel_id=1, source_target_pairs={{0,4},{4,0},{8,12},{12,8},{16,20},{20,16},{24,28},{28,24},{32,36},... | collective-permute-start | bytes 7077896 | tf_op jit(solution)/shard_map/ppermute | solution.py:335
  95.9 51.9 %collective-permute-start.15 = (bf16[768,512]{1,0:T(8,128)(2,1)S(1)}, bf16[768,512]{1,0:T(8,128)(2,1)S(1)}, u32[]{:S(2)}, u32[]{:S(2)}) collective-permute-start(bf16[768,512]{1,0:T(8,128)(2,1)S(1)} %copy-done.1), channel_id=1, source_target_pairs={{0,1},{1,2},{2,3},{3,0},{4,5},{5,6},{6,7},{7,4},{8,9},{9,10},{10,1... | collective-permute-start | bytes 2359304 | tf_op jit(solution)/shard_map/ppermute | solution.py:324
  96.4 51.5 %collective-permute-start.16 = (bf16[768,512]{1,0:T(8,128)(2,1)S(1)}, bf16[768,512]{1,0:T(8,128)(2,1)S(1)}, u32[]{:S(2)}, u32[]{:S(2)}) collective-permute-start(bf16[768,512]{1,0:T(8,128)(2,1)S(1)} %copy-done.1), channel_id=1, source_target_pairs={{0,2},{1,3},{2,0},{3,1},{4,6},{5,7},{6,4},{7,5},{8,10},{9,11},{10,... | collective-permute-start | bytes 2359304 | tf_op jit(solution)/shard_map/ppermute | solution.py:324
  99.8 48.1 %collective-permute-start.17 = (bf16[768,512]{1,0:T(8,128)(2,1)S(1)}, bf16[768,512]{1,0:T(8,128)(2,1)S(1)}, u32[]{:S(2)}, u32[]{:S(2)}) collective-permute-start(bf16[768,512]{1,0:T(8,128)(2,1)S(1)} %copy-done.1), channel_id=1, source_target_pairs={{0,3},{1,0},{2,1},{3,2},{4,7},{5,4},{6,5},{7,6},{8,11},{9,8},{10,9... | collective-permute-start | bytes 2359304 | tf_op jit(solution)/shard_map/ppermute | solution.py:324
  103.6 36.8 %collective-permute-start.13 = (bf16[192,512]{1,0:T(8,128)(2,1)S(1)}, bf16[192,512]{1,0:T(8,128)(2,1)S(1)}, u32[]{:S(2)}, u32[]{:S(2)}) collective-permute-start(bf16[192,512]{1,0:T(8,128)(2,1)S(1)} %copy-done.49), channel_id=1, source_target_pairs={{0,2},{1,3},{2,0},{3,1},{4,6},{5,7},{6,4},{7,5},{8,10},{9,11},{10,... | collective-permute-start | bytes 589832 | tf_op jit(solution)/shard_map/ppermute | solution.py:324
  145.9 135.9 %collective-permute-start.45 = (bf16[4,4,4,48,384]{4,3,2,1,0:T(8,128)(2,1)}, bf16[4,4,4,48,384]{4,3,2,1,0:T(8,128)(2,1)S(1)}, u32[]{:S(2)}, u32[]{:S(2)}) collective-permute-start(bf16[4,4,4,48,384]{4,3,2,1,0:T(8,128)(2,1)} %get-tuple-element.140), channel_id=1, source_target_pairs={{0,4},{4,0},{8,12},{12,8},{16,20},{20,16},{24,28},{28,24},{32,36},... | collective-permute-start | bytes 7077896 | tf_op jit(solution)/shard_map/ppermute | solution.py:335
  230.9 32.4 %collective-permute-start.49 = (bf16[4,4,4,16,384]{4,3,2,1,0:T(8,128)(2,1)}, bf16[4,4,4,16,384]{4,3,2,1,0:T(8,128)(2,1)}, u32[]{:S(2)}, u32[]{:S(2)}) collective-permute-start(bf16[4,4,4,16,384]{4,3,2,1,0:T(8,128)(2,1)} %get-tuple-element.142), channel_id=1, source_target_pairs={{0,4},{4,0},{8,12},{12,8},{16,20},{20,16},{24,28},{28,24},{32,36},... | collective-permute-start | bytes 2359304 | tf_op jit(solution)/shard_map/ppermute | solution.py:335
  236.3 17.2 %collective-permute-start.27 = (bf16[4,4,24,576]{3,2,0,1:T(8,128)(2,1)}, bf16[4,4,24,576]{3,2,0,1:T(8,128)(2,1)}, u32[]{:S(2)}, u32[]{:S(2)}) collective-permute-start(bf16[4,4,24,576]{3,2,0,1:T(8,128)(2,1)} %copy_bitcast_fusion), channel_id=1, source_target_pairs={{0,4},{4,0},{8,12},{12,8},{16,20},{20,16},{24,28},{28,24},{32,36},... | collective-permute-start | bytes 1327112 | tf_op jit(solution)/shard_map/ppermute | solution.py:335
  263.3 21.6 %collective-permute-start.42 = (bf16[4,4,48,384]{3,2,1,0:T(8,128)(2,1)S(1)}, bf16[4,4,48,384]{3,2,1,0:T(8,128)(2,1)S(1)}, u32[]{:S(2)}, u32[]{:S(2)}) collective-permute-start(bf16[4,4,48,384]{3,2,1,0:T(8,128)(2,1)S(1)} %get-tuple-element.177), channel_id=1, source_target_pairs={{0,8},{4,12},{8,16},{12,20},{16,24},{20,28},{24,0},{28,4},{32,40},... | collective-permute-start | bytes 1769480 | tf_op jit(solution)/shard_map/ppermute | solution.py:335
  281.8 21.3 %collective-permute-start.44 = (bf16[4,4,48,384]{3,2,1,0:T(8,128)(2,1)S(1)}, bf16[4,4,48,384]{3,2,1,0:T(8,128)(2,1)S(1)}, u32[]{:S(2)}, u32[]{:S(2)}) collective-permute-start(bf16[4,4,48,384]{3,2,1,0:T(8,128)(2,1)S(1)} %get-tuple-element.175), channel_id=1, source_target_pairs={{0,24},{4,28},{8,0},{12,4},{16,8},{20,12},{24,16},{28,20},{32,56},... | collective-permute-start | bytes 1769480 | tf_op jit(solution)/shard_map/ppermute | solution.py:335
  283.7 19.7 %collective-permute-start.46 = (bf16[4,4,48,384]{3,2,1,0:T(8,128)(2,1)S(1)}, bf16[4,4,48,384]{3,2,1,0:T(8,128)(2,1)S(1)}, u32[]{:S(2)}, u32[]{:S(2)}) collective-permute-start(bf16[4,4,48,384]{3,2,1,0:T(8,128)(2,1)S(1)} %get-tuple-element.173), channel_id=1, source_target_pairs={{0,32},{4,36},{8,40},{12,44},{16,48},{20,52},{24,56},{28,60},{32,6... | collective-permute-start | bytes 1769480 | tf_op jit(solution)/shard_map/ppermute | solution.py:335
  283.7 21.0 %collective-permute-start.47 = (bf16[4,4,48,384]{3,2,1,0:T(8,128)(2,1)S(1)}, bf16[4,4,48,384]{3,2,1,0:T(8,128)(2,1)S(1)}, u32[]{:S(2)}, u32[]{:S(2)}) collective-permute-start(bf16[4,4,48,384]{3,2,1,0:T(8,128)(2,1)S(1)} %get-tuple-element.172), channel_id=1, source_target_pairs={{0,64},{4,68},{8,72},{12,76},{16,80},{20,84},{24,88},{28,92},{32,9... | collective-permute-start | bytes 1769480 | tf_op jit(solution)/shard_map/ppermute | solution.py:335
  284.9 19.8 %collective-permute-start.48 = (bf16[4,4,48,384]{3,2,1,0:T(8,128)(2,1)S(1)}, bf16[4,4,48,384]{3,2,1,0:T(8,128)(2,1)S(1)}, u32[]{:S(2)}, u32[]{:S(2)}) collective-permute-start(bf16[4,4,48,384]{3,2,1,0:T(8,128)(2,1)S(1)} %get-tuple-element.171), channel_id=1, source_target_pairs={{0,96},{4,100},{8,104},{12,108},{16,112},{20,116},{24,120},{28,124... | collective-permute-start | bytes 1769480 | tf_op jit(solution)/shard_map/ppermute | solution.py:335
  291.5 108.3 %collective-permute-start.79 = (f32[8,768]{1,0:T(8,128)S(1)}, f32[8,768]{1,0:T(8,128)S(1)}, u32[]{:S(2)}, u32[]{:S(2)}) collective-permute-start(f32[8,768]{1,0:T(8,128)S(1)} %add_add_fusion), channel_id=1, source_target_pairs={{0,2},{1,3},{2,0},{3,1},{4,6},{5,7},{6,4},{7,5},{8,10},{9,11},{10,... | collective-permute-start | bytes 73736 | tf_op jit(solution)/shard_map/ppermute | solution.py:324
  303.1 96.7 %collective-permute-start.80 = (f32[8,768]{1,0:T(8,128)S(1)}, f32[8,768]{1,0:T(8,128)S(1)}, u32[]{:S(2)}, u32[]{:S(2)}) collective-permute-start(f32[8,768]{1,0:T(8,128)S(1)} %add_add_fusion), channel_id=1, source_target_pairs={{0,1},{1,2},{2,3},{3,0},{4,5},{5,6},{6,7},{7,4},{8,9},{9,10},{10,1... | collective-permute-start | bytes 73736 | tf_op jit(solution)/shard_map/ppermute | solution.py:324
  303.4 27.6 %collective-permute-start.55 = (bf16[4,16,384]{2,1,0:T(8,128)(2,1)S(1)}, bf16[4,16,384]{2,1,0:T(8,128)(2,1)S(1)}, u32[]{:S(2)}, u32[]{:S(2)}) collective-permute-start(bf16[4,16,384]{2,1,0:T(8,128)(2,1)S(1)} %get-tuple-element.199), channel_id=1, source_target_pairs={{0,8},{4,12},{8,16},{12,20},{16,24},{20,28},{24,0},{28,4},{32,40},... | collective-permute-start | bytes 147464 | tf_op jit(solution)/shard_map/ppermute | solution.py:335
  304.7 13.8 %collective-permute-start.56 = (bf16[4,48,384]{2,1,0:T(8,128)(2,1)S(1)}, bf16[4,48,384]{2,1,0:T(8,128)(2,1)S(1)}, u32[]{:S(2)}, u32[]{:S(2)}) collective-permute-start(bf16[4,48,384]{2,1,0:T(8,128)(2,1)S(1)} %get-tuple-element.180), channel_id=1, source_target_pairs={{0,64},{4,68},{8,72},{12,76},{16,80},{20,84},{24,88},{28,92},{32,9... | collective-permute-start | bytes 442376 | tf_op jit(solution)/shard_map/ppermute | solution.py:335
  363.9 35.9 %collective-permute-start.81 = (f32[8,768]{1,0:T(8,128)S(1)}, f32[8,768]{1,0:T(8,128)S(1)}, u32[]{:S(2)}, u32[]{:S(2)}) collective-permute-start(f32[8,768]{1,0:T(8,128)S(1)} %add_add_fusion), channel_id=1, source_target_pairs={{0,3},{1,0},{2,1},{3,2},{4,7},{5,4},{6,5},{7,6},{8,11},{9,8},{10,9... | collective-permute-start | bytes 73736 | tf_op jit(solution)/shard_map/ppermute | solution.py:324
  369.8 41.6 %collective-permute-start.71 = (bf16[4,4,112,384]{3,2,1,0:T(8,128)(2,1)}, bf16[4,4,112,384]{3,2,1,0:T(8,128)(2,1)}, u32[]{:S(2)}, u32[]{:S(2)}) collective-permute-start(bf16[4,4,112,384]{3,2,1,0:T(8,128)(2,1)} %broadcast_select_fusion), channel_id=1, source_target_pairs={{0,4},{4,0},{8,12},{12,8},{16,20},{20,16},{24,28},{28,24},{32,36},... | collective-permute-start | bytes 4128776 | tf_op jit(solution)/shard_map/ppermute | solution.py:335
  (109 other events, 1030.3 us)

commit v2 on v1

v2 whole, which is shorter than its diff:
```python
import jax
import jax.numpy as jnp
from jax import lax
from jax.experimental import pallas as pl
from jax.experimental.pallas import tpu as pltpu
from jax.sharding import PartitionSpec as P

D = 768
HEADS = 12
HD = 64
FF = 3072
PASSES = 5
ROWS = 510
R = 512
EPS = 1e-05
NEG = -1e30
BF = jnp.bfloat16
F32 = jnp.float32
VM = pl.BlockSpec(memory_space=pltpu.VMEM)
SM = pl.BlockSpec(memory_space=pltpu.SMEM)
HB = pl.BlockSpec(memory_space=pl.ANY)
MIB = 1024 * 1024


def room(mib):
    return pltpu.CompilerParams(vmem_limit_bytes=mib * MIB)


def run(kernel, name, mib, outs, operands, scratch=(), scalars=1):
    return pl.pallas_call(
        kernel,
        in_specs=[SM] * scalars + [VM] * (len(operands) - scalars),
        out_specs=[VM] * len(outs),
        out_shape=outs,
        scratch_shapes=list(scratch),
        compiler_params=room(mib),
        name=name,
    )(*operands)


def shape(dims, kind=BF):
    return jax.ShapeDtypeStruct(dims, kind)


def dot(left, right):
    return jnp.dot(left, right, preferred_element_type=F32)


def dot_nt(left, right):
    return lax.dot_general(left, right, (((1,), (1,)), ((), ())), preferred_element_type=F32)


def normalize(values):
    mean = jnp.mean(values, axis=-1, keepdims=True)
    centred = values - mean
    inverse = lax.rsqrt(jnp.mean(centred * centred, axis=-1, keepdims=True) + EPS)
    return centred * inverse, inverse


def norm_back(grad, unit, inverse, gain):
    scaled = grad * gain
    first = jnp.mean(scaled, axis=-1, keepdims=True)
    second = jnp.mean(scaled * unit, axis=-1, keepdims=True)
    return inverse * (scaled - first - unit * second)


def pass_index(blk, count):
    row = lax.broadcasted_iota(jnp.int32, (R, 1), 0) + blk * ROWS
    turns = jnp.floor((row.astype(F32) + 0.5) / count.astype(F32)).astype(jnp.int32)
    return row - turns * count


def pieces_out(stage, outs, blk):
    for d, out in enumerate(outs):
        out[...] = stage[lax.rem(blk + d, 4)]


def project(normed, weights, stage, outs, blk):
    for part, weight in enumerate(weights):
        got = dot(normed, weight[...])
        if part == 0:
            got = got.astype(BF) * jnp.asarray(HD ** (-0.5), BF)
        turned = got.astype(BF).T
        for j in range(4):
            stage[j, 64 * part : 64 * part + 64, :] = turned[64 * j : 64 * j + 64]
    pieces_out(stage, outs, blk)


def first_kernel(
    blk_ref, count_ref, stream, embed, gains, wq, wk, wv, hidden, p0, p1, p2, p3, q0, q1, q2, q3, turned, normed, stage
):
    group = pl.program_id(0)
    blk = blk_ref[0]

    @pl.when(group == 0)
    def _():
        hidden[R - 8 : R, :] = jnp.zeros((8, D), F32)
        hidden[0:ROWS, :] = stream[0].astype(F32)
        which = pass_index(blk, count_ref[0])
        added = embed[0:1, :]
        for r in range(1, PASSES):
            added = jnp.where(which == r, embed[r : r + 1, :], added)
        values = hidden[...] + added
        hidden[...] = values
        unit, _ = normalize(values)
        row = lax.broadcasted_iota(jnp.int32, (R, 1), 0)
        low = jnp.where(row < ROWS, unit * gains[0:1, :], 0.0).astype(BF)
        normed[...] = low
        turned[...] = low.T

    for part, weight in enumerate((wq, wk, wv)):
        got = dot(normed[...], weight[...])
        if part == 0:
            got = got.astype(BF) * jnp.asarray(HD ** (-0.5), BF)
        flipped = got.astype(BF).T
        for j in range(4):
            stage[j, 64 * part : 64 * part + 64, :] = flipped[64 * j : 64 * j + 64]
    for d, (early, late) in enumerate(((p0, q0), (p1, q1), (p2, q2), (p3, q3))):
        piece = stage[lax.rem(blk + d, 4)]

        @pl.when(group == 0)
        def _():
            early[0:192, :] = piece

        @pl.when(group == 1)
        def _():
            early[192:384, :] = piece

        @pl.when(group == 2)
        def _():
            late[...] = piece


def load_heads(blk, at, parts, q_rows, k_rows, v_rows, k_cols):
    for d in range(4):
        s = lax.rem(blk + 4 - d, 4)
        piece = parts[d]
        q_rows[s, 0:64, :] = piece[at : at + 64, :]
        k_rows[s, 0:64, :] = piece[at + 64 : at + 128, :]
        v_rows[s] = piece[at + 128 : at + 192, :]
    row = lax.broadcasted_iota(jnp.int32, (64, R), 0)
    col = lax.broadcasted_iota(jnp.int32, (64, R), 1)
    one = jnp.where(row == 0, 1.0, 0.0).astype(BF)
    off = jnp.where((row == 0) & (col >= ROWS), NEG, 0.0).astype(BF)
    for s in range(4):
        q_rows[s, 64:128, :] = one
        k_rows[s, 64:128, :] = off
    for s in range(4):
        k_cols[s] = k_rows[s].T


def causal():
    key = lax.broadcasted_iota(jnp.int32, (R, R), 0)
    query = lax.broadcasted_iota(jnp.int32, (R, R), 1)
    return key <= query


def attend_kernel(g, blk_ref, r0, r1, r2, r3, *rest):
    last = g == 2
    earlier, rest = (rest[:8], rest[8:]) if last else ((), rest)
    p0, p1, p2, p3, attended, spread, q_rows, k_rows, v_rows, k_cols, scores, stage = rest
    blk = blk_ref[0]
    load_heads(blk, 192 if g == 1 else 0, (r0, r1, r2, r3), q_rows, k_rows, v_rows, k_cols)
    for i in range(4):
        top = None
        for j in range(i + 1):
            got = dot(k_cols[j], q_rows[i])
            if i == j:
                got = jnp.where(causal(), got, NEG)
            scores[j] = got
            best = jnp.max(got, axis=0, keepdims=True)
            top = best if top is None else jnp.maximum(top, best)
        total = jnp.zeros((1, R), F32)
        summed = jnp.zeros((HD, R), F32)
        for j in range(i + 1):
            raised = jnp.exp(scores[j] - top)
            total = total + jnp.sum(raised, axis=0, keepdims=True)
            summed = summed + dot(v_rows[j], raised.astype(BF))
        result = summed / total
        attended[i] = result
        spread[i] = top + jnp.log(total)
        stage[i] = result.astype(BF)
    for d, out in enumerate((p0, p1, p2, p3)):
        piece = stage[lax.rem(blk + d, 4)]
        if last:
            out[0:64, :] = earlier[d][...]
            out[64:128, :] = earlier[4 + d][...]
            out[128:192, :] = piece
        else:
            out[...] = piece


def attend_back_kernel(g, blk_ref, r0, r1, r2, r3, g0, g1, g2, g3, attended, spread, *rest):
    last = g == 2
    if last:
        t0, t1, t2, t3, e0, e1, p0, p1, p2, p3, keep, send, *rest = rest
        outs, made, *rest = rest
    else:
        p0, p1, p2, p3, outs, *rest = rest
    q_rows, k_rows, v_rows, k_cols, q_cols, v_cols, o_rows, o_cols, delta, dq = rest
    blk = blk_ref[0]
    load_heads(blk, 192 if g == 1 else 0, (r0, r1, r2, r3), q_rows, k_rows, v_rows, k_cols)
    for d, piece in enumerate((g0, g1, g2, g3)):
        o_rows[lax.rem(blk + 4 - d, 4)] = piece[...]
    for s in range(4):
        q_cols[s] = q_rows[s].T
        v_cols[s] = v_rows[s].T
        o_cols[s] = o_rows[s].T
        delta[s] = jnp.sum(o_rows[s].astype(F32) * attended[s], axis=0, keepdims=True)
        dq[s] = jnp.zeros((HD, R), F32)
    at = 384 if last else 0
    for j in range(4):
        dk = jnp.zeros((R, 2 * HD), F32)
        dv = jnp.zeros((R, HD), F32)
        for i in range(j, 4):
            got = dot(k_cols[j], q_rows[i])
            if i == j:
                got = jnp.where(causal(), got, NEG)
            probs = jnp.exp(got - spread[i])
            d_probs = dot(v_cols[j], o_rows[i])
            d_scores = (probs * (d_probs - delta[i])).astype(BF)
            dv = dv + dot(probs.astype(BF), o_cols[i])
            dk = dk + dot(d_scores, q_cols[i])
            dq[i] = dq[i] + dot(k_rows[j, 0:64, :], d_scores)
        outs[j, at : at + 64, :] = (dq[j] * HD ** (-0.5)).astype(BF)
        outs[j, at + 64 : at + 128, :] = dk[:, 0:64].astype(BF).T
        outs[j, at + 128 : at + 192, :] = dv.astype(BF).T
    for d, out in enumerate((p0, p1, p2, p3)):
        out[...] = outs[lax.rem(blk + d, 4), at : at + 192, :]
    if last:
        for s in range(4):
            outs[s, 0:192, :] = e0[s]
            outs[s, 192:384, :] = e1[s]
            outs[s, 576:640, :] = jnp.zeros((64, R), BF)
        total = jnp.zeros((D, 640), F32)
        for d, piece in enumerate((t0, t1, t2, t3)):
            total = total + dot_nt(piece[...], outs[lax.rem(blk + 4 - d, 4)])
        made[...] = total
        core = blk_ref[3]
        for i in range(4):
            for xx in range(4):
                for out, c in ((keep, core), (send, 1 - core)):
                    row = pl.multiple_of(192 * i + 24 * xx + 96 * c, 8)
                    part = jnp.concatenate([made[pl.ds(row, 24), :], jnp.zeros((8, 640), F32)], axis=0)
                    out[xx, i] = part.astype(BF)


def gelu_both(value):
    c = (2.0 / jnp.pi) ** 0.5
    square = value * value
    t = jnp.tanh(c * value * (1.0 + 0.044715 * square))
    cdf = 0.5 * (1.0 + t)
    slope = cdf + (0.5 * c) * value * (1.0 - t * t) * (1.0 + 3.0 * 0.044715 * square)
    return value * cdf, slope


CHUNK = 384


def up_cut(values, store):
    for z in range(4):
        for yy in range(4):
            store(yy, z, values[192 * z + 48 * yy : 192 * z + 48 * yy + 48, :])


def down_cut(values, store):
    for yy in range(4):
        for xx in range(4):
            r, col = 48 * (2 * yy + xx // 2), 384 * (xx % 2)
            store(yy, xx, values[r : r + 48, col : col + 384])


def put_block(out, at, rows):
    out[at] = rows.astype(BF)


def ff_kernel(
    blk_ref, r0, r1, r2, r3, hidden, cot, gains, w_out, w_up, w_down,
    active, d_up, second, middle, o_turned, d_branch, d_middle, p0, p1, p2, p3, a_out, b_out, gain_term,
    dy, back, stage, second_turned,
):
    step = pl.program_id(0)
    core = blk_ref[3]

    @pl.when(step == 0)
    def _():
        blk = blk_ref[0]
        for d, piece in enumerate((r0, r1, r2, r3)):
            s = lax.rem(blk + 4 - d, 4)
            for g in range(3):
                stage[4 * g + s] = piece[64 * g : 64 * g + 64, :]
        o_rows = stage[...].reshape(D, R)
        o_turned[...] = o_rows
        values = hidden[...] + dot(o_rows.T, w_out[...])
        middle[...] = values
        unit, _ = normalize(values)
        second[...] = (unit * gains[1:2, :]).astype(BF)
        back[R - 8 : R, :] = jnp.zeros((8, D), F32)
        back[0:ROWS, :] = cot[0].astype(F32)
        dy[...] = back[...].astype(BF)
        back[...] = jnp.zeros((R, D), F32)
        second_turned[...] = second[...].T

    upward = dot(second[...], w_up[...])
    act, slope = gelu_both(upward)
    act = act.astype(BF)
    active[...] = act
    d_active = dot_nt(dy[...], w_down[...])
    d_upward = (d_active * slope).astype(BF)
    d_up[...] = d_upward
    back[...] += dot_nt(d_upward, w_up[...])

    @pl.when(lax.rem(step, 2) != core)
    def _():
        i = step // 2
        up_cut(dot(second_turned[...], d_upward), lambda yy, z, rows: put_block(a_out, (yy, i, z), rows))
        down_cut(dot(act.T, dy[...]), lambda yy, xx, rows: put_block(b_out, (yy, xx, i, slice(0, 48)), rows))

    @pl.when(step == FF // CHUNK - 1)
    def _():
        blk = blk_ref[0]
        unit, inverse = normalize(middle[...])
        grad = back[...]
        gain_term[...] = jnp.sum(grad * unit, axis=0, keepdims=True)
        total = dy[...].astype(F32) + norm_back(grad, unit, inverse, gains[1:2, :])
        d_middle[...] = total
        low = total.astype(BF)
        d_branch[...] = low
        stage[...] = dot_nt(w_out[...], low).astype(BF).reshape(HEADS, HD, R)
        half = dot(o_turned[...], jnp.where(core == 0, low[:, 384:768], low[:, 0:384])).astype(BF)
        for i in range(4):
            for n in range(16):
                rows = half[192 * i + 16 * n : 192 * i + 16 * n + 16, :] if n < 12 else jnp.zeros((16, 384), BF)
                b_out[n // 4, n % 4, i, 48:64] = rows
        for d, out in enumerate((p0, p1, p2, p3)):
            j = lax.rem(blk + d, 4)
            for g in range(3):
                out[64 * g : 64 * g + 64, :] = stage[4 * g + j]


def ff_grad_kernel(
    place_ref, active, d_up, second, cot, o_turned, d_branch, got_a, got_b, a0, a1, a2, a3, b0, b1, b2, b3,
    dy, second_turned, pad, kept, half_out,
):
    step = pl.program_id(0)
    x, y = place_ref[1], place_ref[2]
    chunk = lax.rem(x + step, 4)

    @pl.when(step == 0)
    def _():
        pad[R - 8 : R, :] = jnp.zeros((8, D), F32)
        pad[0:ROWS, :] = cot[0].astype(F32)
        dy[...] = pad[...].astype(BF)
        second_turned[...] = second[...].T
        half_out[...] = dot(o_turned[...], d_branch[...])

    up = dot(second_turned[...], d_up[...])
    down = dot(active[...].T, dy[...])
    for s, out in enumerate((a0, a1, a2, a3)):
        @pl.when(step == s)
        def _():
            up_cut(up, lambda yy, z, rows: put_block(out, (yy, z), rows + got_a[yy, 0, z].astype(F32)))

    def keep_down(yy, xx, rows):
        kept[yy, xx, 0:48] = (rows + got_b[yy, xx, 0, 0:48].astype(F32)).astype(BF)

    down_cut(down, keep_down)
    half = half_out[pl.ds(pl.multiple_of(192 * chunk, 8), 192), :]
    for n in range(16):
        if n < 12:
            rows = half[16 * n : 16 * n + 16, :] + got_b[n // 4, n % 4, 0, 48:64].astype(F32)
            kept[n // 4, n % 4, 48:64] = rows.astype(BF)
        else:
            kept[n // 4, n % 4, 48:64] = jnp.zeros((16, 384), BF)
    for d, out in enumerate((b0, b1, b2, b3)):
        out[:, pl.ds(chunk, 1)] = kept[lax.rem(y + d, 4)][:, None]


def total_of(parts):
    return (parts[0].astype(F32) + parts[2].astype(F32)) + (parts[1].astype(F32) + parts[3].astype(F32))


TINY = 96
GROUP = 160
PART_A = 144
PART_B = 192


def put(buffer, at, block):
    rows, lanes = block.shape
    for t in range(lanes // 128):
        buffer[at + rows * t : at + rows * t + rows, :] = block[:, 128 * t : 128 * t + 128]


def put_small(buffer, at, value):
    high = value.astype(BF)
    low = (value - high.astype(F32)).astype(BF)
    put(buffer, at, jnp.concatenate([high, low], axis=0))


def get_small(buffer, at):
    parts = []
    for t in range(6):
        part = buffer[at + 16 * t : at + 16 * t + 16, :].astype(F32)
        parts.append(part[0:8] + part[8:16])
    return jnp.concatenate(parts, axis=1)


def take(buffer, at, rows):
    return jnp.concatenate([buffer[at + rows * t : at + rows * t + rows, :] for t in range(3)], axis=1)


def cut_kernel(place_ref, a0, a1, a2, a3, b0, b1, b2, b3, keep, got, y0, y1, y2, y3, x0, x1, x2, x3):
    x, y = place_ref[1], place_ref[2]
    for d, (y_out, x_out) in enumerate(((y0, x0), (y1, x1), (y2, x2), (y3, x3))):
        yy, xx = lax.rem(y + d, 4), lax.rem(x + d, 4)
        a_sum = total_of([r[yy] for r in (a0, a1, a2, a3)]).astype(BF)
        heads = (keep[yy].astype(F32) + got[yy].astype(F32)).astype(BF)
        for i in range(4):
            put(y_out, PART_A * i, a_sum[i])
            put(y_out, 4 * PART_A + GROUP * i, heads[i])
        x_out[...] = total_of([r[xx] for r in (b0, b1, b2, b3)]).astype(BF)


def block_kernel(place_ref, y0, y1, y2, y3, x0, x1, x2, x3, small, o0, o1, o2, o3):
    z = place_ref[0]
    for d, out in enumerate((o0, o1, o2, o3)):
        i = lax.rem(z + d, 4)
        start = pl.multiple_of(PART_A * i, 16)
        out[0:PART_A, :] = total_of([r[pl.ds(start, PART_A), :] for r in (y0, y1, y2, y3)]).astype(BF)
        put(out, PART_A, total_of([r[i] for r in (x0, x1, x2, x3)]).astype(BF))
        start = pl.multiple_of(4 * PART_A + GROUP * i, 16)
        at = PART_A + PART_B
        out[at : at + GROUP, :] = total_of([r[pl.ds(start, GROUP), :] for r in (y0, y1, y2, y3)]).astype(BF)
        put_small(out, at + GROUP, small[...])


def own_kernel(place_ref, z0, z1, z2, z3, x_out, y_out):
    parts = (z0, z1, z2, z3)
    at = PART_A + PART_B
    for d, r in enumerate(parts):
        x_out[GROUP * d : GROUP * d + GROUP, :] = r[at : at + GROUP, :]
    put_small(x_out, 4 * GROUP, total_of([get_small(r, at + GROUP) for r in parts]))
    x_out[4 * GROUP + TINY : 4 * GROUP + TINY + PART_A, :] = total_of([r[0:PART_A, :] for r in parts]).astype(BF)
    y_out[...] = total_of([r[PART_A : PART_A + PART_B, :] for r in parts]).astype(BF)


def row_kernel(place_ref, x0, x1, x2, x3, y0, y1, y2, y3, y_out, x_out):
    parts = (x0, x1, x2, x3)
    y_out[0 : 4 * GROUP, :] = total_of([r[0 : 4 * GROUP, :] for r in parts]).astype(BF)
    put_small(y_out, 4 * GROUP, total_of([get_small(r, 4 * GROUP) for r in parts]))
    at = 4 * GROUP + TINY
    for d, (a, b) in enumerate(zip(parts, (y0, y1, y2, y3))):
        y_out[at + PART_A * d : at + PART_A * d + PART_A, :] = a[at : at + PART_A, :]
        x_out[PART_B * d : PART_B * d + PART_B, :] = b[...]


ALL_TINY = 16 * GROUP
ALL_A = ALL_TINY + TINY
ALL_B = ALL_A + 16 * PART_A
ALL = ALL_B + 16 * PART_B


def stack_kernel(place_ref, y0, y1, y2, y3, x0, x1, x2, x3, out):
    parts = (y0, y1, y2, y3)
    put_small(out, ALL_TINY, total_of([get_small(r, 4 * GROUP) for r in parts]))
    at = 4 * GROUP + TINY
    for d, (r, b) in enumerate(zip(parts, (x0, x1, x2, x3))):
        out[4 * GROUP * d : 4 * GROUP * d + 4 * GROUP, :] = r[0 : 4 * GROUP, :]
        out[ALL_A + 4 * PART_A * d : ALL_A + 4 * PART_A * d + 4 * PART_A, :] = r[at : at + 4 * PART_A, :]
        out[ALL_B + 4 * PART_B * d : ALL_B + 4 * PART_B * d + 4 * PART_B, :] = b[...]


def finish_kernel(place_ref, mine, other, grad_qkv, grad_out, grad_up, grad_down, gains, passes, pair, turned):
    z, x, y, core = place_ref[0], place_ref[1], place_ref[2], place_ref[3]
    pair[core] = mine[...]
    pair[1 - core] = other[...]

    def rows(c, at, count):
        return pair[c, pl.ds(pl.multiple_of(at, 16), count), :].astype(F32)

    for c in range(2):
        for xx in range(4):
            dx = lax.rem(x + 4 - xx, 4)
            for yy in range(4):
                dy = lax.rem(y + 4 - yy, 4)
                a = rows(c, ALL_A + 4 * PART_A * dy + PART_A * dx, PART_A)
                b = rows(c, ALL_B + 4 * PART_B * dx + PART_B * dy, PART_B)
                r = 384 * c + 48 * (2 * yy + xx // 2)
                for t in range(3):
                    col = 384 * (2 * xx + c) + 128 * t
                    grad_up[48 * yy : 48 * yy + 48, col : col + 128] = a[48 * t : 48 * t + 48]
                    col = 384 * (xx % 2) + 128 * t
                    grad_down[r : r + 48, col : col + 128] = b[64 * t : 64 * t + 48]
                    if yy < 3:
                        n, col = 16 * (4 * yy + xx), 384 * c + 128 * t
                        grad_out[n : n + 16, col : col + 128] = b[64 * t + 48 : 64 * t + 64]
        for yy in range(4):
            dy = lax.rem(y + 4 - yy, 4)
            for j in range(4):
                dz = lax.rem(z + 4 - j, 4)
                piece = rows(c, 4 * GROUP * dy + GROUP * dz, GROUP)
                r = 96 * c + 24 * yy
                for n in range(9):
                    lane = 64 * n
                    block = piece[32 * (lane // 128) : 32 * (lane // 128) + 24, lane % 128 : lane % 128 + 64]
                    col = D * (n % 3) + 64 * (4 * (n // 3) + j)
                    grad_qkv[r : r + 24, col : col + 64] = block
    small = get_small(mine, ALL_TINY) + get_small(other, ALL_TINY)
    turned[...] = small.T
    part = turned[pl.ds(pl.multiple_of(192 * z, 8), 192), :]
    gains[...] = part[:, 0:2]
    passes[...] = part[:, 2:7]


def layer_out_kernel(place_ref, middle, active, w_down, out, total):
    step = pl.program_id(0)

    @pl.when(step == 0)
    def _():
        total[...] = middle[...]

    total[...] += dot(active[...], w_down[...])

    @pl.when(step == FF // CHUNK - 1)
    def _():
        out[0] = total[0:ROWS, :].astype(BF)


def input_grad_kernel(blk_ref, a0, a1, a2, a3, b0, b1, b2, b3, w_qkv, out, stage):
    blk = blk_ref[0]
    stage[...] = jnp.zeros((36, HD, R), BF)
    for g, group in enumerate(((a0, a1, a2, a3), (b0, b1, b2, b3))):
        for d, piece in enumerate(group):
            s = lax.rem(blk + 4 - d, 4)
            for part in range(3):
                stage[12 * part + 4 * g + s] = piece[64 * part : 64 * part + 64, :]
    out[...] = dot(w_qkv[...], stage[...].reshape(3 * D, R))


def last_kernel(
    blk_ref, count_ref, c0, c1, c2, c3, so_far, hidden, d_middle, gain_term, gains, wq, wk, wv, grad_stream, small, stage
):
    blk = blk_ref[0]
    for d, piece in enumerate((c0, c1, c2, c3)):
        s = lax.rem(blk + 4 - d, 4)
        for part in range(3):
            stage[part, s] = piece[64 * part : 64 * part + 64, :]
    turned = so_far[...]
    for part, weight in enumerate((wq, wk, wv)):
        turned = turned + dot(weight[...], stage[part].reshape(256, R))
    grad = turned.T
    unit, inverse = normalize(hidden[...])
    total = d_middle[...] + norm_back(grad, unit, inverse, gains[0:1, :])
    grad_stream[0] = total[0:ROWS, :]
    row = lax.broadcasted_iota(jnp.int32, (R, 1), 0)
    which = jnp.where(row < ROWS, pass_index(blk, count_ref[0]), -1)
    small[0:1, :] = jnp.sum(grad * unit, axis=0, keepdims=True)
    small[1:2, :] = gain_term[...]
    for r in range(PASSES):
        small[2 + r : 3 + r, :] = jnp.sum(jnp.where(which == r, total, 0.0), axis=0, keepdims=True)
    small[7:8, :] = jnp.zeros((1, D), F32)


def shift(values, axis, d):
    if axis == "z":
        return lax.ppermute(values, "blk", [(i, (i + d) % 4) for i in range(4)])
    pairs = []
    for b in range(32):
        y, x, core = b // 8, (b // 2) % 4, b % 2
        if axis == "y":
            y = (y + d) % 4
        elif axis == "x":
            x = (x + d) % 4
        else:
            core = (core + d) % 2
        pairs.append((b, 8 * y + 2 * x + core))
    return lax.ppermute(values, "batch", pairs)


def spread_pieces(pieces, axis):
    return (pieces[0],) + tuple(shift(pieces[d], axis, d) for d in (1, 2, 3))


def all_of(value, axis):
    return spread_pieces((value,) * 4, axis)


def after(value, *others):
    return lax.optimization_barrier((value,) + others)[0]


def far(value):
    return pltpu.with_memory_space_constraint(value, pltpu.HBM)


def weight_spec(column):
    return pl.BlockSpec((D, 256), lambda *_, column=column: (0, column))


def on_device(stream, cotangent, passes, w_qkv, w_out, w_up, w_down, ln_gains, pass_embed):
    z = lax.axis_index("blk").astype(jnp.int32)
    batch = lax.axis_index("batch").astype(jnp.int32)
    place = jnp.stack([z, batch // 2 % 4, batch // 8, batch % 2])
    gains = ln_gains.T
    embed = pass_embed.T
    piece = shape((192, R))
    full = shape((R, D))

    def arrived(*values):
        nonlocal place
        place = lax.optimization_barrier((place,) + values)[0]

    def ordered(outs):
        nonlocal place
        *outs, first = outs
        place, first = lax.optimization_barrier((place, first))
        return (*outs, first)

    hidden, *sent, turned = ordered(pl.pallas_call(
        first_kernel,
        grid=(3,),
        in_specs=[SM, SM, VM, VM, VM, *(pl.BlockSpec((D, 256), lambda g, part=part: (0, 3 * part + g)) for part in range(3))],
        out_specs=[VM] * 10,
        out_shape=[shape((R, D), F32)] + [shape((384, R))] * 4 + [piece] * 4 + [shape((D, R))],
        scratch_shapes=[pltpu.VMEM((R, D), BF), pltpu.VMEM((4, 192, R), BF)],
        compiler_params=room(24),
        name="ln_qkv",
    )(place, passes, far(stream), embed, gains, *([far(w_qkv)] * 3)))
    early, late = spread_pieces(sent[:4], "z"), spread_pieces(sent[4:], "z")
    heads = (early, early, late)

    attended, spreads, sent = [], [], []
    for g in range(3):
        *parts, result, spread = ordered(run(
            lambda *refs, g=g: attend_kernel(g, *refs),
            "attend",
            24,
            [shape((192 if g == 2 else HD, R))] * 4 + [shape((4, HD, R), F32), shape((4, 1, R), F32)],
            (place, *(far(h) for h in heads[g]), *(sent if g == 2 else ())),
            [
                pltpu.VMEM((4, 128, R), BF),
                pltpu.VMEM((4, 128, R), BF),
                pltpu.VMEM((4, HD, R), BF),
                pltpu.VMEM((4, R, 128), BF),
                pltpu.VMEM((4, R, R), F32),
                pltpu.VMEM((4, HD, R), BF),
            ],
        ))
        attended.append(result)
        spreads.append(spread)
        sent += parts
    back_o = spread_pieces(sent[8:], "z")
    near = after(turned, *back_o)
    near = (shift(near, "z", 1), shift(near, "z", 3))

    active, d_up, second, middle, o_turned, d_branch, d_middle, *sent, a_other, b_other, gain_term = ordered(pl.pallas_call(
        ff_kernel,
        grid=(FF // CHUNK,),
        in_specs=[SM] + [VM] * 4 + [VM, VM, VM, VM]
        + [pl.BlockSpec((D, CHUNK), lambda f: (0, f)), pl.BlockSpec((CHUNK, D), lambda f: (f, 0))],
        out_specs=[pl.BlockSpec((R, CHUNK), lambda f: (0, f)), pl.BlockSpec((R, CHUNK), lambda f: (0, f))] + [VM] * 12,
        out_shape=[shape((R, FF)), shape((R, FF)), full, shape((R, D), F32), shape((D, R)), full, shape((R, D), F32)]
        + [piece] * 4 + [shape((4, 4, 4, 48, 384)), shape((4, 4, 4, 64, 384)), shape((1, D), F32)],
        scratch_shapes=[pltpu.VMEM((R, D), BF), pltpu.VMEM((R, D), F32), pltpu.VMEM((HEADS, HD, R), BF), pltpu.VMEM((D, R), BF)],
        compiler_params=room(36),
        name="ff",
    )(place, *(far(o) for o in back_o), far(hidden), far(cotangent), gains, far(w_out), far(w_up), far(w_down)))
    *sent, a_other, b_other = lax.optimization_barrier((*sent, a_other, b_other, *near))[:6]
    d_o = spread_pieces(sent, "z")

    got = (shift(a_other, "core", 1), shift(b_other, "core", 1))
    layer_out = ordered((pl.pallas_call(
        layer_out_kernel,
        grid=(FF // CHUNK,),
        in_specs=[SM, VM, pl.BlockSpec((R, CHUNK), lambda f: (0, f)), pl.BlockSpec((CHUNK, D), lambda f: (f, 0))],
        out_specs=VM,
        out_shape=shape((1, ROWS, D)),
        scratch_shapes=[pltpu.VMEM((R, D), F32)],
        compiler_params=room(16),
        name="layer_out",
    )(place, middle, active, far(w_down)),))[0]
    arrived(*d_o)
    distant = shift(after(turned, *d_o, place), "z", 2)

    def chunk(i, s):
        return (0, 2 * lax.rem(s[1] + i, 4) + s[3])

    def at_chunk(axis):
        return lambda i, s: tuple(lax.rem(s[1] + i, 4) if n == axis else 0 for n in range(5))

    sent = ordered(pl.pallas_call(
        ff_grad_kernel,
        grid_spec=pltpu.PrefetchScalarGridSpec(
            num_scalar_prefetch=1,
            grid=(4,),
            in_specs=[
                pl.BlockSpec((R, 384), chunk),
                pl.BlockSpec((R, 384), chunk),
                VM,
                VM,
                VM,
                pl.BlockSpec((R, 384), lambda i, s: (0, s[3])),
                pl.BlockSpec((4, 1, 4, 48, 384), at_chunk(1)),
                pl.BlockSpec((4, 4, 1, 64, 384), at_chunk(2)),
            ],
            out_specs=[VM] * 8,
            scratch_shapes=[
                pltpu.VMEM((R, D), BF),
                pltpu.VMEM((D, R), BF),
                pltpu.VMEM((R, D), F32),
                pltpu.VMEM((4, 4, 64, 384), BF),
                pltpu.VMEM((D, 384), F32),
            ],
        ),
        out_shape=[shape((4, 4, 48, 384))] * 4 + [shape((4, 4, 64, 384))] * 4,
        compiler_params=room(32),
        name="ff_grad",
    )(place, active, d_up, second, far(cotangent), o_turned, d_branch, *(far(t) for t in got)))
    a_sent, b_sent = sent[0:4], sent[4:8]
    a_parts = [a_sent[0], shift(a_sent[1], "x", 1), None, shift(a_sent[3], "x", 3)]
    b_parts = [b_sent[0], shift(b_sent[1], "y", 1), None, shift(b_sent[3], "y", 3)]

    def attend_back(g):
        last = g == 2
        scratch = [
            pltpu.VMEM((4, 128, R), BF),
            pltpu.VMEM((4, 128, R), BF),
            pltpu.VMEM((4, HD, R), BF),
            pltpu.VMEM((4, R, 128), BF),
            pltpu.VMEM((4, R, 128), BF),
            pltpu.VMEM((4, R, HD), BF),
            pltpu.VMEM((4, HD, R), BF),
            pltpu.VMEM((4, R, HD), BF),
            pltpu.VMEM((4, 1, R), F32),
            pltpu.VMEM((4, HD, R), F32),
        ]
        if last:
            scratch = [pltpu.VMEM((4, 640, R), BF), pltpu.VMEM((D, 640), F32)] + scratch
            extra = (far(turned), far(near[0]), far(distant), far(near[1]), far(made[0]), far(made[1]))
        else:
            extra = ()
        return ordered(pl.pallas_call(
            lambda *refs, g=g: attend_back_kernel(g, *refs),
            grid=(1,),
            in_specs=[SM] + [VM] * 4 + [pl.BlockSpec((HD, R), lambda _, g=g: (g, 0))] * 4 + [VM] * (2 + len(extra)),
            out_specs=[VM] * (6 if last else 5),
            out_shape=[piece] * 4 + ([shape((4, 4, 32, 640))] * 2 if last else [shape((4, 192, R))]),
            scratch_shapes=scratch,
            compiler_params=room(32 if last else 24),
            name="attend_back",
        )(place, *(far(h) for h in heads[g]), *(far(t) for t in d_o), far(attended[g]), far(spreads[g]), *extra))

    pieces, made = [], []
    *sent, one = attend_back(0)
    made.append(one)
    pieces.append(spread_pieces(sent, "z"))
    a_parts[2] = shift(after(a_sent[2], place), "x", 2)
    b_parts[2] = shift(after(b_sent[2], place), "y", 2)
    arrived(a_parts[1], a_parts[3], b_parts[1], b_parts[3], distant)
    *sent, one = attend_back(1)
    made.append(one)
    pieces.append(spread_pieces(sent, "z"))
    arrived(*pieces[0])
    *sent, keep, send = attend_back(2)
    *sent, send = lax.optimization_barrier((*sent, send, *pieces[1], a_parts[2], b_parts[2]))[:5]
    pieces.append(spread_pieces(sent, "z"))
    got = shift(send, "core", 1)
    arrived(*pieces[1], a_parts[2], b_parts[2])

    so_far = ordered(run(
        input_grad_kernel,
        "input_grad",
        24,
        [shape((D, R), F32)],
        (place, *(far(p) for p in pieces[0] + pieces[1]), far(w_qkv)),
        [pltpu.VMEM((36, HD, R), BF)],
    ))[0]
    sent = ordered(run(
        cut_kernel,
        "sum_first",
        24,
        [shape((4 * PART_A + 4 * GROUP, 128))] * 4 + [shape((4, 64, 384))] * 4,
        (place, *(far(t) for t in a_parts + b_parts), far(keep), far(got)),
    ))
    y_parts, x_parts = spread_pieces(sent[0:4], "y"), spread_pieces(sent[4:8], "x")
    grad_stream, small = ordered(pl.pallas_call(
        last_kernel,
        grid=(1,),
        in_specs=[SM, SM] + [VM] * 9 + [weight_spec(c) for c in (2, 5, 8)],
        out_specs=[VM, VM],
        out_shape=[shape((1, ROWS, D), F32), shape((8, D), F32)],
        scratch_shapes=[pltpu.VMEM((3, 4, HD, R), BF)],
        compiler_params=room(24),
        name="ln_back",
    )(place, passes, *(far(p) for p in pieces[2]), so_far, far(hidden), far(d_middle), gain_term, gains, *([far(w_qkv)] * 3)))
    sent = ordered(run(
        block_kernel,
        "sum_second",
        16,
        [shape((PART_A + PART_B + GROUP + TINY, 128))] * 4,
        (place, *(far(t) for t in y_parts + x_parts), small),
    ))
    buffers = ordered(run(
        own_kernel,
        "sum_blocks",
        16,
        [shape((4 * GROUP + TINY + PART_A, 128)), shape((PART_B, 128))],
        (place, *(far(t) for t in spread_pieces(sent, "z"))),
    ))
    buffers = ordered(run(
        row_kernel,
        "stack_rows",
        16,
        [shape((4 * GROUP + TINY + 4 * PART_A, 128)), shape((4 * PART_B, 128))],
        (place, *(far(t) for t in all_of(buffers[0], "x") + all_of(buffers[1], "y"))),
    ))
    buffer = ordered(run(
        stack_kernel,
        "stack",
        16,
        [shape((ALL, 128))],
        (place, *(far(t) for t in all_of(buffers[0], "y") + all_of(buffers[1], "x"))),
    ))[0]
    results = run(
        finish_kernel,
        "finish",
        32,
        [
            shape((192, 3 * D), F32),
            shape((192, D), F32),
            shape((192, FF), F32),
            shape((D, D), F32),
            shape((192, 2), F32),
            shape((192, PASSES), F32),
        ],
        (place, far(buffer), far(shift(buffer, "core", 1))),
        [pltpu.VMEM((2, ALL, 128), BF), pltpu.VMEM((D, 8), F32)],
    )
    return (layer_out, grad_stream, *results)


def solution(mesh):
    tokens = P("batch", "blk", None)
    in_specs = (tokens, tokens, P("batch"), P(), P(), P(), P(), P(), P())
    out_specs = (tokens, tokens) + (P("blk", None),) * 6
    return jax.shard_map(on_device, mesh=mesh, in_specs=in_specs, out_specs=out_specs, check_vma=False)
```

time: 430 us -> 297 us (0.69)
  waiting for transfers between devices: 138 us -> 45 us
  other arithmetic: 22.3 us -> 0.08 us
  starting transfers between devices: 118 us -> 101 us
    ppermute x36 -> x27, waiting for transfers between devices: 80 us -> 26.9 us  [shift(): return lax.ppermute(values, 'blk', [(i, (i + d) % 4) for i in range(4)])]
    ppermute x46 -> x28, waiting for transfers between devices: 58.5 us -> 18.1 us  [shift(): return lax.ppermute(values, 'batch', pairs)]
    unnamed x111 -> x177, local copies, waits for them, and re-layouts: 10.4 us -> 25.5 us
    ppermute x46 -> x28, starting transfers between devices: 79.3 us -> 65 us  [shift(): return lax.ppermute(values, 'batch', pairs)]
    convert_element_type x9 -> x0, other arithmetic: 10.8 us -> none  [the longest x4 6.44 us: scatter_sum(): sum((pick(t, index, dim).astype(F32) for t in terms)).astype(BF)]
    pallas_call x1, Pallas kernels: 18.7 us -> 24 us  [on_device(): pl.pallas_call(ff_kernel, grid=(FF // CHUNK,), in_specs=[SM] + [VM] * 4 +...]
    convert_element_type x2 -> x0, local copies, waits for them, and re-layouts: 5.23 us -> none  [on_device(): grad_qkv = got.reshape(192, 3 * D).astype(F32)]
    gather x6 -> x0, local copies, waits for them, and re-layouts: 4.35 us -> none  [the longest x3 2.24 us: on_device(): jnp.take(got, lax.rem(z + 4 - jnp.arange(4, dtype=jnp.int32), 4), axis=2)]
  transfers between devices with their start and end apart: 82 -> 55, of which waited for: 39 -> 19; matrix products, arithmetic and copies ran while one was open for 8% -> 1% of each run, Pallas kernels for 17% -> 32%
where the time goes in v2:
time: 297 us; the launch traced here: 293 us
  Pallas kernels  118 us (40%)
  starting transfers between devices  101 us (34%)
  waiting for transfers between devices  45 us (15%)
  local copies, waits for them, and re-layouts  25.5 us (9%)
    ppermute x28, starting transfers between devices, shift(): return lax.ppermute(values, 'batch', pairs)  65 us
    ppermute x27, starting transfers between devices, shift(): return lax.ppermute(values, 'blk', [(i, (i + d) % 4) for i in range(4)])  36.5 us
    pallas_call x10, Pallas kernels, run(): pl.pallas_call(kernel, in_specs=[SM] * scalars + [VM] * (len(operands) -...  36.3 us
    pallas_call x3, Pallas kernels, attend_back(): pl.pallas_call(lambda *refs, g=g: attend_back_kernel(g, *refs), grid=(1,)...  30.2 us
    ppermute x27, waiting for transfers between devices, shift(): return lax.ppermute(values, 'blk', [(i, (i + d) % 4) for i in range(4)])  26.9 us
    unnamed x177, local copies, waits for them, and re-layouts  25.5 us
    pallas_call x1, Pallas kernels, on_device(): pl.pallas_call(ff_kernel, grid=(FF // CHUNK,), in_specs=[SM] + [VM] * 4 +...  24 us
    ppermute x28, waiting for transfers between devices, shift(): return lax.ppermute(values, 'batch', pairs)  18.1 us
  transfers between devices with their start and end apart: 55, of which 19 were waited for; matrix products, arithmetic and copies ran while one was open for 1% of the time, Pallas kernels for 32%

profile of v2, /device:TPU:1, one launch (start us, length us, event | category | flops | bytes accessed | tf_op | source)
XLA Modules:
  0.0 293.0 jit_solution(2919745117812205092)
XLA Ops:
  2.8 6.0 %ln_qkv.1 = (f32[512,768]{1,0:T(8,128)S(1)}, bf16[384,512]{1,0:T(8,128)(2,1)S(1)}, bf16[384,512]{1,0:T(8,128)(2,1)S(1)}, bf16[384,512]{1,0:T(8,128)(2,1)S(1)}, b...) custom-call(s32[4]{0:T(128)S(1)} %pad_add_fusion.blk_ref.refs_0_.pla, ...), custom_call_target="tpu_custom_call" | custom-call | tf_op jit(solution)/shard_map/ln_qkv/pallas_call | solution.py:620
  13.2 3.3 %collective-permute-start.1 = (bf16[384,512]{1,0:T(8,128)(2,1)S(1)}, bf16[384,512]{1,0:T(8,128)(2,1)S(1)}, u32[]{:S(2)}, u32[]{:S(2)}) collective-permute-start(bf16[384,512]{1,0:T(8,128)(2,1)S(1)} %get-tuple-element.155), channel_id=1, source_target_pairs={{0,2},{1,3},{2,0},{3,1},{4,6},{5,7},{6,4},{7,5},{8,10},{9,11},{10,... | collective-permute-start | bytes 1179656 | tf_op jit(solution)/shard_map/ppermute | solution.py:567
  18.4 5.7 %collective-permute-done.refs_2_ = bf16[384,512]{1,0:T(8,128)(2,1)S(1)} collective-permute-done((bf16[384,512]{1,0:T(8,128)(2,1)S(1)}, bf16[384,512]{1,0:T(8,128)(2,1)S(1)}, u32[]{:S(2)}, u32[]{:S(2)}) %collective-permute-start) | collective-permute-done | bytes 393248 | tf_op jit(solution)/shard_map/ppermute | solution.py:567
  25.4 8.0 %collective-permute-done.1.refs_3_ = bf16[384,512]{1,0:T(8,128)(2,1)S(1)} collective-permute-done((bf16[384,512]{1,0:T(8,128)(2,1)S(1)}, bf16[384,512]{1,0:T(8,128)(2,1)S(1)}, u32[]{:S(2)}, u32[]{:S(2)}) %collective-permute-start.1) | collective-permute-done | bytes 393248 | tf_op jit(solution)/shard_map/ppermute | solution.py:567
  34.3 5.3 %attend.3 = (bf16[64,512]{1,0:T(8,128)(2,1)S(1)}, bf16[64,512]{1,0:T(8,128)(2,1)S(1)}, bf16[64,512]{1,0:T(8,128)(2,1)S(1)}, bf16[64,512]{1,0:T(8,128)(2,1)S(1)},...) custom-call(s32[4]{0:T(128)S(1)} %pad_add_fusion.blk_ref.refs_0_.place_ref, bf16[384,512]{1,0:T(8,128)(2,1)} %copy-done.1, ...), custom_call_target="tpu_custom_call" | custom-call | tf_op jit(solution)/shard_map/attend/pallas_call | solution.py:30
  41.1 5.3 %attend.4 = (bf16[64,512]{1,0:T(8,128)(2,1)S(1)}, bf16[64,512]{1,0:T(8,128)(2,1)S(1)}, bf16[64,512]{1,0:T(8,128)(2,1)S(1)}, bf16[64,512]{1,0:T(8,128)(2,1)S(1)},...) custom-call(s32[4]{0:T(128)S(1)} %pad_add_fusion.blk_ref.refs_0_.place_ref, bf16[384,512]{1,0:T(8,128)(2,1)} %copy-done.1, ...), custom_call_target="tpu_custom_call" | custom-call | tf_op jit(solution)/shard_map/attend/pallas_call | solution.py:30
  48.1 5.2 %attend.5 = (bf16[192,512]{1,0:T(8,128)(2,1)S(1)}, bf16[192,512]{1,0:T(8,128)(2,1)S(1)}, bf16[192,512]{1,0:T(8,128)(2,1)S(1)}, bf16[192,512]{1,0:T(8,128)(2,1)S(...) custom-call(s32[4]{0:T(128)S(1)} %pad_add_fusion.blk_ref.refs_0_.place_ref, bf16[192,512]{1,0:T(8,128)(2,1)} %copy-done.5, ...), custom_call_target="tpu_custom_call" | custom-call | tf_op jit(solution)/shard_map/attend/pallas_call | solution.py:30
  61.6 6.6 %collective-permute-done.7.r2 = bf16[192,512]{1,0:T(8,128)(2,1)S(1)} collective-permute-done((bf16[192,512]{1,0:T(8,128)(2,1)S(1)}, bf16[192,512]{1,0:T(8,128)(2,1)S(1)}, u32[]{:S(2)}, u32[]{:S(2)}) %collective-permute-start.7) | collective-permute-done | bytes 196640 | tf_op jit(solution)/shard_map/ppermute | solution.py:567
  71.0 24.0 %ff.1 = (bf16[512,3072]{1,0:T(8,128)(2,1)S(1)}, bf16[512,3072]{1,0:T(8,128)(2,1)S(1)}, bf16[512,768]{1,0:T(8,128)(2,1)S(1)}, f32[512,768]{1,0:T(8,128)S(1)}, bf1...) custom-call(s32[4]{0:T(128)S(1)} %pad_add_fusion.blk_ref.refs_0_.pla, ...), custom_call_target="tpu_custom_call" | custom-call | tf_op jit(solution)/shard_map/ff/pallas_call | solution.py:657
  100.1 8.6 %layer_out.1 = bf16[1,510,768]{2,1,0:T(8,128)(2,1)} custom-call(s32[4]{0:T(128)S(1)} %pad_add_fusion.blk_ref.refs_0_.place_ref, f32[512,768]{1,0:T(8,128)S(1)} %get-tuple-element.182.middle, bf16[512,3072]{1,0:T(8,128)(2,1)S(1)} %get-tuple-element.183.active, bf16[3072,768]{1,0:T(8,128)(2,1)} %w_down.3), custom_call_target="tpu_custom_call" | custom-call | tf_op jit(solution)/shard_map/layer_out/pallas_call | solution.py:673
  113.7 8.2 %ff_grad.1 = (bf16[4,4,48,384]{3,2,1,0:T(8,128)(2,1)S(1)}, bf16[4,4,48,384]{3,2,1,0:T(8,128)(2,1)S(1)}, bf16[4,4,48,384]{3,2,1,0:T(8,128)(2,1)S(1)}, bf16[4,4,48...) custom-call(s32[4]{0:T(128)S(1)} %pad_add_fusion.blk_ref.refs_0_.pla, ...), custom_call_target="tpu_custom_call" | custom-call | tf_op jit(solution)/shard_map/ff_grad/pallas_call | solution.py:692
  128.5 8.6 %attend_back.3 = (bf16[192,512]{1,0:T(8,128)(2,1)S(1)}, bf16[192,512]{1,0:T(8,128)(2,1)S(1)}, bf16[192,512]{1,0:T(8,128)(2,1)S(1)}, bf16[192,512]{1,0:T(8,128)(2,1)S(1)}, bf16[4,192,512]{2,1,0:T(8,128)(2,1)S(1)}) custom-call(s32[4]{0:T(128)S(1)} %pad_add_fusion.blk_ref.refs_0_.place_ref, bf16[384,512]{1,0:T(8,128)(2,1)} %copy-done.1, ...), custom_call_target="tpu_custom_call" | custom-call | tf_op jit(solution)/shard_map/attend_back/pallas_call | solution.py:743
  145.9 8.6 %attend_back.4 = (bf16[192,512]{1,0:T(8,128)(2,1)S(1)}, bf16[192,512]{1,0:T(8,128)(2,1)S(1)}, bf16[192,512]{1,0:T(8,128)(2,1)S(1)}, bf16[192,512]{1,0:T(8,128)(2,1)S(1)}, bf16[4,192,512]{2,1,0:T(8,128)(2,1)S(1)}) custom-call(s32[4]{0:T(128)S(1)} %pad_add_fusion.blk_ref.refs_0_.place_ref, bf16[384,512]{1,0:T(8,128)(2,1)} %copy-done.1, ...), custom_call_target="tpu_custom_call" | custom-call | tf_op jit(solution)/shard_map/attend_back/pallas_call | solution.py:743
  159.2 12.9 %attend_back.5 = (bf16[192,512]{1,0:T(8,128)(2,1)S(1)}, bf16[192,512]{1,0:T(8,128)(2,1)S(1)}, bf16[192,512]{1,0:T(8,128)(2,1)S(1)}, bf16[192,512]{1,0:T(8,128)(2...) custom-call(s32[4]{0:T(128)S(1)} %pad_add_fusion.blk_ref.refs_0_.place_ref, ...), custom_call_target="tpu_custom_call" | custom-call | tf_op jit(solution)/shard_map/attend_back/pallas_call | solution.py:743
  172.2 5.6 %collective-permute-start.29 = (bf16[4,4,32,640]{3,2,1,0:T(8,128)(2,1)S(1)}, bf16[4,4,32,640]{3,2,1,0:T(8,128)(2,1)S(1)}, u32[]{:S(2)}, u32[]{:S(2)}) collective-permute-start(bf16[4,4,32,640]{3,2,1,0:T(8,128)(2,1)S(1)} %get-tuple-element.250), channel_id=1, source_target_pairs={{0,4},{4,0},{8,12},{12,8},{16,20},{20,16},{24,28},{28,24},{32,36},... | collective-permute-start | bytes 1966088 | tf_op jit(solution)/shard_map/ppermute | solution.py:578
  179.0 4.8 %input_grad.1.so_far = f32[768,512]{1,0:T(8,128)S(1)} custom-call(s32[4]{0:T(128)S(1)} %pad_add_fusion.blk_ref.refs_0_.place_ref, bf16[192,512]{1,0:T(8,128)(2,1)} %copy-done.21, bf16[192,512]{1,0:T(8,128)(2,1)} %copy-done.72, bf16[192,512]{1,0:T(8,128)(2,1)} %copy-done.73, bf16[192,512]{1,0:T(8,128)(2,1)} %copy-done.74, bf16[192,512]{1,0:T(8,128)(2,1)} %copy-done.22, ...), custom_call_target="tpu_custom_call" | custom-call | tf_op jit(solution)/shard_map/input_grad/pallas_call | solution.py:30
  186.9 3.8 %sum_first.1 = (bf16[1216,128]{1,0:T(8,128)(2,1)S(1)}, bf16[1216,128]{1,0:T(8,128)(2,1)S(1)}, bf16[1216,128]{1,0:T(8,128)(2,1)S(1)}, bf16[1216,128]{1,0:T(8,128)...) custom-call(s32[4]{0:T(128)S(1)} %pad_add_fusion.blk_ref.refs_0_.pla, ...), custom_call_target="tpu_custom_call" | custom-call | tf_op jit(solution)/shard_map/sum_first/pallas_call | solution.py:30
  193.4 18.1 %collective-permute-start.34 = (bf16[1216,128]{1,0:T(8,128)(2,1)S(1)}, bf16[1216,128]{1,0:T(8,128)(2,1)S(1)}, u32[]{:S(2)}, u32[]{:S(2)}) collective-permute-start(bf16[1216,128]{1,0:T(8,128)(2,1)S(1)} %get-tuple-element.265), channel_id=1, source_target_pairs={{0,64},{4,68},{8,72},{12,76},{16,80},{20,84},{24,88},{28,92},{32,9... | collective-permute-start | bytes 933896 | tf_op jit(solution)/shard_map/ppermute | solution.py:578
  215.9 5.0 %ln_back.1 = (f32[1,510,768]{2,1,0:T(8,128)S(1)}, f32[8,768]{1,0:T(8,128)S(1)}) custom-call(s32[4]{0:T(128)S(1)} %pad_add_fusion.blk_ref.refs_0_.place_ref, s32[1]{0:T(128)S(6)} %copy.20.count_ref, bf16[192,512]{1,0:T(8,128)(2,1)} %copy-done.18, bf16[192,512]{1,0:T(8,128)(2,1)} %copy-done.63, bf16[192,512]{1,0:T(8,128)(2,1)} %copy-done.64, ...), custom_call_target="tpu_custom_call" | custom-call | tf_op jit(solution)/shard_map/ln_back/pallas_call | solution.py:787
  231.3 3.7 %collective-permute-done.39.z1 = bf16[592,128]{1,0:T(8,128)(2,1)S(1)} collective-permute-done((bf16[592,128]{1,0:T(8,128)(2,1)S(1)}, bf16[592,128]{1,0:T(8,128)(2,1)S(1)}, u32[]{:S(2)}, u32[]{:S(2)}) %collective-permute-start.39) | collective-permute-done | bytes 151584 | tf_op jit(solution)/shard_map/ppermute | solution.py:567
  244.0 3.5 %collective-permute-start.46 = (bf16[192,128]{1,0:T(8,128)(2,1)S(1)}, bf16[192,128]{1,0:T(8,128)(2,1)S(1)}, u32[]{:S(2)}, u32[]{:S(2)}) collective-permute-start(bf16[192,128]{1,0:T(8,128)(2,1)S(1)} %get-tuple-element.281.y0), channel_id=1, source_target_pairs={{0,64},{4,68},{8,72},{12,76},{16,80},{20,84},{24,88},{28,92},{32,9... | collective-permute-start | bytes 147464 | tf_op jit(solution)/shard_map/ppermute | solution.py:578
  256.7 4.0 %collective-permute-start.49 = (bf16[1312,128]{1,0:T(8,128)(2,1)S(1)}, bf16[1312,128]{1,0:T(8,128)(2,1)S(1)}, u32[]{:S(2)}, u32[]{:S(2)}) collective-permute-start(bf16[1312,128]{1,0:T(8,128)(2,1)S(1)} %get-tuple-element.284.y0), channel_id=1, source_target_pairs={{0,64},{4,68},{8,72},{12,76},{16,80},{20,84},{24,88},{28,92},{32,9... | collective-permute-start | bytes 1007624 | tf_op jit(solution)/shard_map/ppermute | solution.py:578
  268.8 4.6 %collective-permute-done.49.y2 = bf16[1312,128]{1,0:T(8,128)(2,1)S(1)} collective-permute-done((bf16[1312,128]{1,0:T(8,128)(2,1)S(1)}, bf16[1312,128]{1,0:T(8,128)(2,1)S(1)}, u32[]{:S(2)}, u32[]{:S(2)}) %collective-permute-start.49) | collective-permute-done | bytes 335904 | tf_op jit(solution)/shard_map/ppermute | solution.py:578
  285.3 5.9 %finish.1 = (f32[192,2304]{1,0:T(8,128)}, f32[192,768]{1,0:T(8,128)}, f32[192,3072]{1,0:T(8,128)}, f32[768,768]{1,0:T(8,128)}, f32[192,2]{1,0:T(8,128)S(1)}, /*index=5*/f32[192,5]{1,0:T(8,128)S(1)}) custom-call(s32[4]{0:T(128)S(1)} %pad_add_fusion.blk_ref.refs_0_.place_ref, bf16[8032,128]{1,0:T(8,128)(2,1)} %copy-done, bf16[8032,128]{1,0:T(8,128)(2,1)} %copy-done.37), custom_call_target="tpu_custom_call" | custom-call | tf_op jit(solution)/shard_map/finish/pallas_call | solution.py:30
  (282 shorter events, 115.1 us)
Async XLA Ops:
  13.2 20.3 %collective-permute-start.1 = (bf16[384,512]{1,0:T(8,128)(2,1)S(1)}, bf16[384,512]{1,0:T(8,128)(2,1)S(1)}, u32[]{:S(2)}, u32[]{:S(2)}) collective-permute-start(bf16[384,512]{1,0:T(8,128)(2,1)S(1)} %get-tuple-element.155), channel_id=1, source_target_pairs={{0,2},{1,3},{2,0},{3,1},{4,6},{5,7},{6,4},{7,5},{8,10},{9,11},{10,... | collective-permute-start | bytes 1179656 | tf_op jit(solution)/shard_map/ppermute | solution.py:567
  16.5 17.0 %collective-permute-start.2 = (bf16[384,512]{1,0:T(8,128)(2,1)S(1)}, bf16[384,512]{1,0:T(8,128)(2,1)S(1)}, u32[]{:S(2)}, u32[]{:S(2)}) collective-permute-start(bf16[384,512]{1,0:T(8,128)(2,1)S(1)} %get-tuple-element.156), channel_id=1, source_target_pairs={{0,3},{1,0},{2,1},{3,2},{4,7},{5,4},{6,5},{7,6},{8,11},{9,8},{10,9... | collective-permute-start | bytes 1179656 | tf_op jit(solution)/shard_map/ppermute | solution.py:567
  17.2 30.0 %collective-permute-start.3 = (bf16[192,512]{1,0:T(8,128)(2,1)S(1)}, bf16[192,512]{1,0:T(8,128)(2,1)S(1)}, u32[]{:S(2)}, u32[]{:S(2)}) collective-permute-start(bf16[192,512]{1,0:T(8,128)(2,1)S(1)} %get-tuple-element.162), channel_id=1, source_target_pairs={{0,1},{1,2},{2,3},{3,0},{4,5},{5,6},{6,7},{7,4},{8,9},{9,10},{10,1... | collective-permute-start | bytes 589832 | tf_op jit(solution)/shard_map/ppermute | solution.py:567
  17.9 29.3 %collective-permute-start.4 = (bf16[192,512]{1,0:T(8,128)(2,1)S(1)}, bf16[192,512]{1,0:T(8,128)(2,1)S(1)}, u32[]{:S(2)}, u32[]{:S(2)}) collective-permute-start(bf16[192,512]{1,0:T(8,128)(2,1)S(1)} %get-tuple-element.163), channel_id=1, source_target_pairs={{0,2},{1,3},{2,0},{3,1},{4,6},{5,7},{6,4},{7,5},{8,10},{9,11},{10,... | collective-permute-start | bytes 589832 | tf_op jit(solution)/shard_map/ppermute | solution.py:567
  24.1 23.1 %collective-permute-start.5 = (bf16[192,512]{1,0:T(8,128)(2,1)S(1)}, bf16[192,512]{1,0:T(8,128)(2,1)S(1)}, u32[]{:S(2)}, u32[]{:S(2)}) collective-permute-start(bf16[192,512]{1,0:T(8,128)(2,1)S(1)} %get-tuple-element.164), channel_id=1, source_target_pairs={{0,3},{1,0},{2,1},{3,2},{4,7},{5,4},{6,5},{7,6},{8,11},{9,8},{10,9... | collective-permute-start | bytes 589832 | tf_op jit(solution)/shard_map/ppermute | solution.py:567
  68.2 26.8 %collective-permute-start.9 = (bf16[768,512]{1,0:T(8,128)(2,1)S(1)}, bf16[768,512]{1,0:T(8,128)(2,1)S(1)}, u32[]{:S(2)}, u32[]{:S(2)}) collective-permute-start(bf16[768,512]{1,0:T(8,128)(2,1)S(1)} %get-tuple-element.215.refs_11_), channel_id=1, source_target_pairs={{0,1},{1,2},{2,3},{3,0},{4,5},{5,6},{6,7},{7,4},{8,9},{9,10},{10,1... | collective-permute-start | bytes 2359304 | tf_op jit(solution)/shard_map/ppermute | solution.py:567
  68.3 26.7 %collective-permute-start.10 = (bf16[768,512]{1,0:T(8,128)(2,1)S(1)}, bf16[768,512]{1,0:T(8,128)(2,1)S(1)}, u32[]{:S(2)}, u32[]{:S(2)}) collective-permute-start(bf16[768,512]{1,0:T(8,128)(2,1)S(1)} %get-tuple-element.215.refs_11_), channel_id=1, source_target_pairs={{0,3},{1,0},{2,1},{3,2},{4,7},{5,4},{6,5},{7,6},{8,11},{9,8},{10,9... | collective-permute-start | bytes 2359304 | tf_op jit(solution)/shard_map/ppermute | solution.py:567
  95.0 16.1 %collective-permute-start.15 = (bf16[4,4,4,64,384]{4,3,2,1,0:T(8,128)(2,1)S(1)}, bf16[4,4,4,64,384]{4,3,2,1,0:T(8,128)(2,1)S(1)}, u32[]{:S(2)}, u32[]{:S(2)}) collective-permute-start(bf16[4,4,4,64,384]{4,3,2,1,0:T(8,128)(2,1)S(1)} %get-tuple-element.204), channel_id=1, source_target_pairs={{0,4},{4,0},{8,12},{12,8},{16,20},{20,16},{24,28},{28,24},{32,36},... | collective-permute-start | bytes 9437192 | tf_op jit(solution)/shard_map/ppermute | solution.py:578
  109.2 28.6 %collective-permute-start.20 = (bf16[768,512]{1,0:T(8,128)(2,1)S(1)}, bf16[768,512]{1,0:T(8,128)(2,1)S(1)}, u32[]{:S(2)}, u32[]{:S(2)}) collective-permute-start(bf16[768,512]{1,0:T(8,128)(2,1)S(1)} %get-tuple-element.215.refs_11_), channel_id=1, source_target_pairs={{0,2},{1,3},{2,0},{3,1},{4,6},{5,7},{6,4},{7,5},{8,10},{9,11},{10,... | collective-permute-start | bytes 2359304 | tf_op jit(solution)/shard_map/ppermute | solution.py:567
  122.7 19.7 %collective-permute-start.18 = (bf16[4,4,64,384]{3,2,1,0:T(8,128)(2,1)S(1)}, bf16[4,4,64,384]{3,2,1,0:T(8,128)(2,1)S(1)}, u32[]{:S(2)}, u32[]{:S(2)}) collective-permute-start(bf16[4,4,64,384]{3,2,1,0:T(8,128)(2,1)S(1)} %get-tuple-element.213), channel_id=1, source_target_pairs={{0,32},{4,36},{8,40},{12,44},{16,48},{20,52},{24,56},{28,60},{32,6... | collective-permute-start | bytes 2359304 | tf_op jit(solution)/shard_map/ppermute | solution.py:578
  124.0 15.5 %collective-permute-start.16 = (bf16[4,4,48,384]{3,2,1,0:T(8,128)(2,1)S(1)}, bf16[4,4,48,384]{3,2,1,0:T(8,128)(2,1)S(1)}, u32[]{:S(2)}, u32[]{:S(2)}) collective-permute-start(bf16[4,4,48,384]{3,2,1,0:T(8,128)(2,1)S(1)} %get-tuple-element.211), channel_id=1, source_target_pairs={{0,8},{4,12},{8,16},{12,20},{16,24},{20,28},{24,0},{28,4},{32,40},... | collective-permute-start | bytes 1769480 | tf_op jit(solution)/shard_map/ppermute | solution.py:578
  125.2 18.5 %collective-permute-start.19 = (bf16[4,4,64,384]{3,2,1,0:T(8,128)(2,1)S(1)}, bf16[4,4,64,384]{3,2,1,0:T(8,128)(2,1)S(1)}, u32[]{:S(2)}, u32[]{:S(2)}) collective-permute-start(bf16[4,4,64,384]{3,2,1,0:T(8,128)(2,1)S(1)} %get-tuple-element.214), channel_id=1, source_target_pairs={{0,96},{4,100},{8,104},{12,108},{16,112},{20,116},{24,120},{28,124... | collective-permute-start | bytes 2359304 | tf_op jit(solution)/shard_map/ppermute | solution.py:578
  137.8 34.4 %collective-permute-start.28 = (bf16[4,4,64,384]{3,2,1,0:T(8,128)(2,1)S(1)}, bf16[4,4,64,384]{3,2,1,0:T(8,128)(2,1)S(1)}, u32[]{:S(2)}, u32[]{:S(2)}) collective-permute-start(bf16[4,4,64,384]{3,2,1,0:T(8,128)(2,1)S(1)} %get-tuple-element.239), channel_id=1, source_target_pairs={{0,64},{4,68},{8,72},{12,76},{16,80},{20,84},{24,88},{28,92},{32,9... | collective-permute-start | bytes 2359304 | tf_op jit(solution)/shard_map/ppermute | solution.py:578
  139.5 32.7 %collective-permute-start.27 = (bf16[4,4,48,384]{3,2,1,0:T(8,128)(2,1)S(1)}, bf16[4,4,48,384]{3,2,1,0:T(8,128)(2,1)S(1)}, u32[]{:S(2)}, u32[]{:S(2)}) collective-permute-start(bf16[4,4,48,384]{3,2,1,0:T(8,128)(2,1)S(1)} %get-tuple-element.237), channel_id=1, source_target_pairs={{0,16},{4,20},{8,24},{12,28},{16,0},{20,4},{24,8},{28,12},{32,48},... | collective-permute-start | bytes 1769480 | tf_op jit(solution)/shard_map/ppermute | solution.py:578
  141.0 15.2 %collective-permute-start.21 = (bf16[192,512]{1,0:T(8,128)(2,1)S(1)}, bf16[192,512]{1,0:T(8,128)(2,1)S(1)}, u32[]{:S(2)}, u32[]{:S(2)}) collective-permute-start(bf16[192,512]{1,0:T(8,128)(2,1)S(1)} %get-tuple-element.222), channel_id=1, source_target_pairs={{0,1},{1,2},{2,3},{3,0},{4,5},{5,6},{6,7},{7,4},{8,9},{9,10},{10,1... | collective-permute-start | bytes 589832 | tf_op jit(solution)/shard_map/ppermute | solution.py:567
  156.2 16.0 %collective-permute-start.24 = (bf16[192,512]{1,0:T(8,128)(2,1)S(1)}, bf16[192,512]{1,0:T(8,128)(2,1)S(1)}, u32[]{:S(2)}, u32[]{:S(2)}) collective-permute-start(bf16[192,512]{1,0:T(8,128)(2,1)S(1)} %get-tuple-element.233), channel_id=1, source_target_pairs={{0,1},{1,2},{2,3},{3,0},{4,5},{5,6},{6,7},{7,4},{8,9},{9,10},{10,1... | collective-permute-start | bytes 589832 | tf_op jit(solution)/shard_map/ppermute | solution.py:567
  156.2 16.0 %collective-permute-start.25 = (bf16[192,512]{1,0:T(8,128)(2,1)S(1)}, bf16[192,512]{1,0:T(8,128)(2,1)S(1)}, u32[]{:S(2)}, u32[]{:S(2)}) collective-permute-start(bf16[192,512]{1,0:T(8,128)(2,1)S(1)} %get-tuple-element.234), channel_id=1, source_target_pairs={{0,2},{1,3},{2,0},{3,1},{4,6},{5,7},{6,4},{7,5},{8,10},{9,11},{10,... | collective-permute-start | bytes 589832 | tf_op jit(solution)/shard_map/ppermute | solution.py:567
  177.8 15.5 %collective-permute-start.30 = (bf16[192,512]{1,0:T(8,128)(2,1)S(1)}, bf16[192,512]{1,0:T(8,128)(2,1)S(1)}, u32[]{:S(2)}, u32[]{:S(2)}) collective-permute-start(bf16[192,512]{1,0:T(8,128)(2,1)S(1)} %get-tuple-element.254), channel_id=1, source_target_pairs={{0,1},{1,2},{2,3},{3,0},{4,5},{5,6},{6,7},{7,4},{8,9},{9,10},{10,1... | collective-permute-start | bytes 589832 | tf_op jit(solution)/shard_map/ppermute | solution.py:567
  177.9 33.6 %collective-permute-start.31 = (bf16[192,512]{1,0:T(8,128)(2,1)S(1)}, bf16[192,512]{1,0:T(8,128)(2,1)S(1)}, u32[]{:S(2)}, u32[]{:S(2)}) collective-permute-start(bf16[192,512]{1,0:T(8,128)(2,1)S(1)} %get-tuple-element.255), channel_id=1, source_target_pairs={{0,2},{1,3},{2,0},{3,1},{4,6},{5,7},{6,4},{7,5},{8,10},{9,11},{10,... | collective-permute-start | bytes 589832 | tf_op jit(solution)/shard_map/ppermute | solution.py:567
  183.8 28.5 %collective-permute-start.32 = (bf16[192,512]{1,0:T(8,128)(2,1)S(1)}, bf16[192,512]{1,0:T(8,128)(2,1)S(1)}, u32[]{:S(2)}, u32[]{:S(2)}) collective-permute-start(bf16[192,512]{1,0:T(8,128)(2,1)S(1)} %get-tuple-element.256), channel_id=1, source_target_pairs={{0,3},{1,0},{2,1},{3,2},{4,7},{5,4},{6,5},{7,6},{8,11},{9,8},{10,9... | collective-permute-start | bytes 589832 | tf_op jit(solution)/shard_map/ppermute | solution.py:567
  191.4 23.4 %collective-permute-start.36 = (bf16[4,64,384]{2,1,0:T(8,128)(2,1)S(1)}, bf16[4,64,384]{2,1,0:T(8,128)(2,1)S(1)}, u32[]{:S(2)}, u32[]{:S(2)}) collective-permute-start(bf16[4,64,384]{2,1,0:T(8,128)(2,1)S(1)} %get-tuple-element.268), channel_id=1, source_target_pairs={{0,8},{4,12},{8,16},{12,20},{16,24},{20,28},{24,0},{28,4},{32,40},... | collective-permute-start | bytes 589832 | tf_op jit(solution)/shard_map/ppermute | solution.py:578
  192.6 28.9 %collective-permute-start.33 = (bf16[1216,128]{1,0:T(8,128)(2,1)S(1)}, bf16[1216,128]{1,0:T(8,128)(2,1)S(1)}, u32[]{:S(2)}, u32[]{:S(2)}) collective-permute-start(bf16[1216,128]{1,0:T(8,128)(2,1)S(1)} %get-tuple-element.264), channel_id=1, source_target_pairs={{0,32},{4,36},{8,40},{12,44},{16,48},{20,52},{24,56},{28,60},{32,6... | collective-permute-start | bytes 933896 | tf_op jit(solution)/shard_map/ppermute | solution.py:578
  193.4 30.9 %collective-permute-start.34 = (bf16[1216,128]{1,0:T(8,128)(2,1)S(1)}, bf16[1216,128]{1,0:T(8,128)(2,1)S(1)}, u32[]{:S(2)}, u32[]{:S(2)}) collective-permute-start(bf16[1216,128]{1,0:T(8,128)(2,1)S(1)} %get-tuple-element.265), channel_id=1, source_target_pairs={{0,64},{4,68},{8,72},{12,76},{16,80},{20,84},{24,88},{28,92},{32,9... | collective-permute-start | bytes 933896 | tf_op jit(solution)/shard_map/ppermute | solution.py:578
  256.7 16.7 %collective-permute-start.49 = (bf16[1312,128]{1,0:T(8,128)(2,1)S(1)}, bf16[1312,128]{1,0:T(8,128)(2,1)S(1)}, u32[]{:S(2)}, u32[]{:S(2)}) collective-permute-start(bf16[1312,128]{1,0:T(8,128)(2,1)S(1)} %get-tuple-element.284.y0), channel_id=1, source_target_pairs={{0,64},{4,68},{8,72},{12,76},{16,80},{20,84},{24,88},{28,92},{32,9... | collective-permute-start | bytes 1007624 | tf_op jit(solution)/shard_map/ppermute | solution.py:578
  (118 other events, 1196.1 us)
